TPU v7x, 32 devices: a whole 2x2x4 slice. The times are simulated.
32 devices in a mesh: ctx: 16 (over z, y, x), fsdp: 2 (over core).
Axes of the slice: x: 2, y: 2, z: 4, core: 2. Of those that a mesh axis runs over, the one named last changes fastest.
Arguments:
- block_input: bfloat16 [2, 2048, 1088], P('fsdp', 'ctx'), may hold values from -6 to 6
- cotangent: bfloat16 [2, 2048, 1088], P('fsdp', 'ctx'), may hold values from -6 to 6
- block_order: int32 [32], replicated, may hold values from 0 to 31, each once
- gain_in: bfloat16 [1088], P('fsdp'), may hold values from 0.099609375 to 1.8984375
- shift_in: bfloat16 [1088], P('fsdp'), may hold values from -3 to 3
- w_qkv: bfloat16 [1088, 3264], P('fsdp'), may hold values from -0.1875 to 0.1875
- qv_bias: bfloat16 [2176], P('fsdp'), may hold values from -3 to 3
- w_out: bfloat16 [1088, 1088], P('fsdp'), may hold values from -3 to 3
- out_bias: bfloat16 [1088], P('fsdp'), may hold values from -3 to 3
- gain_mid: bfloat16 [1088], P('fsdp'), may hold values from 0.099609375 to 1.8984375
- shift_mid: bfloat16 [1088], P('fsdp'), may hold values from -3 to 3
- w_fc: bfloat16 [1088, 4352], P('fsdp'), may hold values from -0.1875 to 0.1875
- fc_bias: bfloat16 [4352], P('fsdp'), may hold values from -3 to 3
- w_down: bfloat16 [1088, 4352], P('fsdp'), may hold values from -0.09375 to 0.09375
- down_bias: bfloat16 [1088], P('fsdp'), may hold values from -3 to 3
Outputs:
- block_output: bfloat16 [2, 2048, 1088], P('fsdp', 'ctx')
- grad_block_input: float32 [2, 2048, 1088], P('fsdp', 'ctx')
- grad_gain_in: float32 [1088], P('fsdp')
- grad_shift_in: float32 [1088], P('fsdp')
- grad_w_qkv: float32 [1088, 3264], P('fsdp', 'ctx')
- grad_qv_bias: float32 [2176], P('fsdp')
- grad_w_out: float32 [1088, 1088], P('fsdp', 'ctx')
- grad_out_bias: float32 [1088], P('fsdp')
- grad_gain_mid: float32 [1088], P('fsdp')
- grad_shift_mid: float32 [1088], P('fsdp')
- grad_w_fc: float32 [1088, 4352], P('fsdp', 'ctx')
- grad_fc_bias: float32 [4352], P('fsdp')
- grad_w_down: float32 [1088, 4352], P('fsdp', 'ctx')
- grad_down_bias: float32 [1088], P('fsdp')
Inputs may be any that keep to these rules, and one draw needn't show every extreme that they name: block_order holds each of the 32 blocks of positions exactly once.
All inputs are finite; a program needn't handle non-finite values.
Results may differ from a plain program's by a relative error of at most 0.013.
Values may be sent and summed in bfloat16 or wider, within the bound.
A program may use at most 320 MiB of HBM per device.

v0:
```python
import math

import jax
import jax.numpy as jnp
from jax import lax
from jax.sharding import PartitionSpec as P

HEAD_DIM = 64


epsilon = 1e-05
gelu_scale = 0.7978845608028654
gelu_cubic = 0.044715


def from_behind(shard, axis, by):
    size = lax.axis_size(axis)
    return lax.ppermute(shard, axis, [(i, (i + by) % size) for i in range(size)])


def layer_norm(inputs, gain_vec, shift_vec):
    average = jnp.mean(inputs, axis=-1, keepdims=True)
    centred = inputs - average
    variance = jnp.mean(centred * centred, axis=-1, keepdims=True)
    inv_std = lax.rsqrt(variance + epsilon)
    normed = centred * inv_std
    return (normed * gain_vec + shift_vec, normed, inv_std)


def norm_back(upstream, normed, inv_std, gain_vec):
    scaled = upstream * gain_vec
    mean_scaled = jnp.mean(scaled, axis=-1, keepdims=True)
    mean_cross = jnp.mean(scaled * normed, axis=-1, keepdims=True)
    return inv_std * (scaled - mean_scaled - normed * mean_cross)


def gelu_parts(pre_act):
    inner = gelu_scale * (pre_act + gelu_cubic * pre_act * pre_act * pre_act)
    tangent = jnp.tanh(inner)
    value_act = 0.5 * pre_act * (1.0 + tangent)
    slope = 0.5 * (1.0 + tangent) + 0.5 * pre_act * (1.0 - tangent * tangent) * gelu_scale * (
        1.0 + 3.0 * gelu_cubic * pre_act * pre_act
    )
    return (value_act, slope)


def block_positions(block_order, first_row, row_count, half_block):
    row_ids = first_row + jnp.arange(row_count, dtype=jnp.int32)
    block_ids = row_ids // half_block
    table_ids = jnp.arange(block_order.shape[0], dtype=jnp.int32)
    one_hot = (block_ids[:, None] == table_ids[None, :]).astype(jnp.int32)
    return jnp.sum(one_hot * block_order[None, :], axis=1) * half_block + row_ids % half_block


def over_blocks(update, carry, pieces, block_order, half_block, empty_test):
    row_count = pieces[0].shape[0]
    step_rows = math.gcd(row_count, 512)
    step_count = row_count // step_rows
    stacked = tuple(
        (member.reshape((step_count, step_rows) + member.shape[1:]) for member in pieces)
    )

    def advance(carried, scan_item):
        block_index, parts = scan_item
        first_row = block_index * step_rows
        piece_pos = block_positions(block_order, first_row, step_rows, half_block)
        carried = lax.cond(
            empty_test(piece_pos),
            lambda unchanged: unchanged,
            lambda current: update(current, parts, piece_pos, first_row),
            carried,
        )
        return (carried, None)

    final_state, trailing = lax.scan(
        advance, carry, (jnp.arange(step_count, dtype=jnp.int32), stacked)
    )
    return final_state


def local(
    block_input,
    cotangent,
    block_order,
    gain_in,
    shift_in,
    w_qkv,
    qv_bias,
    w_out,
    out_bias,
    gain_mid,
    shift_mid,
    w_fc,
    fc_bias,
    w_down,
    down_bias,
):
    tokens = block_input.shape[1]
    model_width = block_input.shape[2]
    head_count = model_width // HEAD_DIM
    half_block = tokens // 2
    factor = 1.0 / math.sqrt(HEAD_DIM)
    cycle_count = lax.axis_size("ctx")
    gathered = (
        lax.all_gather(gain_in, "fsdp", axis=0, tiled=True),
        lax.all_gather(shift_in, "fsdp", axis=0, tiled=True),
        lax.all_gather(w_qkv, "fsdp", axis=0, tiled=True),
        lax.all_gather(qv_bias, "fsdp", axis=0, tiled=True),
        lax.all_gather(w_out, "fsdp", axis=0, tiled=True),
        lax.all_gather(out_bias, "fsdp", axis=0, tiled=True),
        lax.all_gather(gain_mid, "fsdp", axis=0, tiled=True),
        lax.all_gather(shift_mid, "fsdp", axis=0, tiled=True),
        lax.all_gather(w_fc, "fsdp", axis=0, tiled=True),
        lax.all_gather(fc_bias, "fsdp", axis=0, tiled=True),
        lax.all_gather(w_down, "fsdp", axis=0, tiled=True),
        lax.all_gather(down_bias, "fsdp", axis=0, tiled=True),
    )
    (
        gain_in_full,
        shift_in_full,
        qkv_full,
        qv_full,
        out_full,
        bias_out_full,
        gain_mid_full,
        shift_mid_full,
        fc_full,
        bias_fc_full,
        down_full,
        bias_down_full,
    ) = gathered
    gain_one = gain_in_full.astype(jnp.float32)
    gain_two = gain_mid_full.astype(jnp.float32)
    device_slot = lax.axis_index("ctx")
    query_pos = block_positions(block_order, device_slot * tokens, tokens, half_block)
    top_query = jnp.max(query_pos)

    def later_keys(key_pos):
        return jnp.min(key_pos) > top_query

    inputs = block_input.reshape(tokens, model_width)
    wide_in = inputs.astype(jnp.float32)
    hidden_in, normed_in, inv_in = layer_norm(wide_in, gain_one, shift_in_full.astype(jnp.float32))
    act_in = hidden_in.astype(jnp.bfloat16)
    bias_full = jnp.concatenate(
        [
            qv_full[:model_width].astype(jnp.float32),
            jnp.zeros((model_width,), jnp.float32),
            qv_full[model_width:].astype(jnp.float32),
        ]
    )
    qkv_rows = jnp.dot(act_in, qkv_full, preferred_element_type=jnp.float32) + bias_full
    queries = qkv_rows[:, :model_width].astype(jnp.bfloat16).reshape(tokens, head_count, HEAD_DIM)
    keys_own = (
        qkv_rows[:, model_width : 2 * model_width]
        .astype(jnp.bfloat16)
        .reshape(tokens, head_count, HEAD_DIM)
    )
    values_own = (
        qkv_rows[:, 2 * model_width :].astype(jnp.bfloat16).reshape(tokens, head_count, HEAD_DIM)
    )

    def forward_update(carried, parts, key_pos, first_row):
        row_max, row_total, value_sum = carried
        key_rows, value_rows = parts
        scores = (
            jnp.einsum("qhe,khe->hqk", queries, key_rows, preferred_element_type=jnp.float32)
            * factor
        )
        allowed = key_pos[None, None, :] <= query_pos[None, :, None]
        scores = jnp.where(allowed, scores, -1e30)
        new_max = jnp.maximum(row_max, jnp.max(scores, axis=-1))
        soft_weights = jnp.where(allowed, jnp.exp(scores - new_max[:, :, None]), 0.0)
        rescale = jnp.exp(row_max - new_max)
        row_total = row_total * rescale + jnp.sum(soft_weights, axis=-1)
        value_sum = value_sum * jnp.transpose(rescale)[:, :, None] + jnp.einsum(
            "hqk,khe->qhe",
            soft_weights.astype(jnp.bfloat16),
            value_rows,
            preferred_element_type=jnp.float32,
        )
        return (new_max, row_total, value_sum)

    init_max = jnp.full((head_count, tokens), -1e30, jnp.float32)
    init_total = jnp.zeros((head_count, tokens), jnp.float32)
    init_sum = jnp.zeros((tokens, head_count, HEAD_DIM), jnp.float32)
    row_max, row_total, value_sum = over_blocks(
        forward_update,
        (init_max, init_total, init_sum),
        (
            lax.all_gather(keys_own, "ctx", axis=0, tiled=True),
            lax.all_gather(values_own, "ctx", axis=0, tiled=True),
        ),
        block_order,
        half_block,
        later_keys,
    )
    attended = value_sum / jnp.transpose(row_total)[:, :, None]
    log_rows = jnp.transpose(row_max + jnp.log(row_total))
    attended_bf = attended.reshape(tokens, model_width).astype(jnp.bfloat16)
    residual = (
        wide_in
        + jnp.dot(attended_bf, out_full, preferred_element_type=jnp.float32)
        + bias_out_full.astype(jnp.float32)
    )
    hidden_mid, normed_mid, inv_mid = layer_norm(
        residual, gain_two, shift_mid_full.astype(jnp.float32)
    )
    act_mid = hidden_mid.astype(jnp.bfloat16)
    pre_act = jnp.dot(act_mid, fc_full, preferred_element_type=jnp.float32) + bias_fc_full.astype(
        jnp.float32
    )
    value_act, slope = gelu_parts(pre_act)
    act_ff = value_act.astype(jnp.bfloat16)
    result = (
        residual
        + jnp.dot(act_ff, down_full.T, preferred_element_type=jnp.float32)
        + bias_down_full.astype(jnp.float32)
    ).astype(jnp.bfloat16)
    qkv_back, out_back, fc_back, down_back = (qkv_full, out_full, fc_full, down_full)
    upstream = cotangent.reshape(tokens, model_width)
    up_wide = upstream.astype(jnp.float32)
    grad_down_bias = jnp.sum(up_wide, axis=0)
    grad_pre = jnp.dot(upstream, down_back, preferred_element_type=jnp.float32) * slope
    grad_fc_bias = jnp.sum(grad_pre, axis=0)
    grad_pre_bf = grad_pre.astype(jnp.bfloat16)
    grad_norm_mid = jnp.dot(grad_pre_bf, fc_back.T, preferred_element_type=jnp.float32)
    grad_gain_mid = jnp.sum(grad_norm_mid * normed_mid, axis=0)
    grad_shift_mid = jnp.sum(grad_norm_mid, axis=0)
    grad_res = up_wide + norm_back(grad_norm_mid, normed_mid, inv_mid, gain_two)
    grad_out_bias = jnp.sum(grad_res, axis=0)
    grad_res_bf = grad_res.astype(jnp.bfloat16)
    grad_heads = (
        jnp.dot(grad_res_bf, out_back.T, preferred_element_type=jnp.float32)
        .astype(jnp.bfloat16)
        .reshape(tokens, head_count, HEAD_DIM)
    )
    delta_rows = jnp.sum(grad_heads.astype(jnp.float32) * attended, axis=-1)
    zeros_kv = jnp.zeros((tokens, head_count, HEAD_DIM), jnp.float32)
    log_heads = jnp.transpose(log_rows)
    delta_heads = jnp.transpose(delta_rows)

    def cycle_update(inner, key_rows, value_rows, key_pos):
        acc_key, acc_value, acc_query = inner
        scores = (
            jnp.einsum("qhe,khe->hqk", queries, key_rows, preferred_element_type=jnp.float32)
            * factor
        )
        allowed = key_pos[None, None, :] <= query_pos[None, :, None]
        soft_weights = jnp.where(allowed, jnp.exp(scores - log_heads[:, :, None]), 0.0)
        grad_soft = jnp.einsum(
            "qhe,khe->hqk", grad_heads, value_rows, preferred_element_type=jnp.float32
        )
        grad_score = soft_weights * (grad_soft - delta_heads[:, :, None])
        score_bf = grad_score.astype(jnp.bfloat16)
        weight_bf = soft_weights.astype(jnp.bfloat16)
        acc_query = (
            acc_query
            + jnp.einsum("hqk,khe->qhe", score_bf, key_rows, preferred_element_type=jnp.float32)
            * factor
        )
        acc_key = (
            acc_key
            + jnp.einsum("hqk,qhe->khe", score_bf, queries, preferred_element_type=jnp.float32)
            * factor
        )
        acc_value = acc_value + jnp.einsum(
            "hqk,qhe->khe", weight_bf, grad_heads, preferred_element_type=jnp.float32
        )
        return (acc_key, acc_value, acc_query)

    def cycle_step(step, state):
        key_rows, value_rows, acc_key, acc_value, acc_query = state
        source = (device_slot - step) % cycle_count
        key_pos = block_positions(block_order, source * tokens, tokens, half_block)
        inner = (acc_key, acc_value, acc_query)
        inner = lax.cond(
            later_keys(key_pos),
            lambda unchanged: unchanged,
            lambda current: cycle_update(current, key_rows, value_rows, key_pos),
            inner,
        )
        moved_kv = from_behind((key_rows, value_rows), "ctx", 1)
        moved_grads = from_behind((inner[0], inner[1]), "ctx", 1)
        return (moved_kv[0], moved_kv[1], moved_grads[0], moved_grads[1], inner[2])

    final_state = lax.fori_loop(
        0, cycle_count, cycle_step, (keys_own, values_own, zeros_kv, zeros_kv, zeros_kv)
    )
    grad_key = final_state[2]
    grad_value = final_state[3]
    grad_query = final_state[4]
    grad_query = grad_query.reshape(tokens, model_width)
    grad_value = grad_value.reshape(tokens, model_width)
    grad_qv_bias = jnp.concatenate([jnp.sum(grad_query, axis=0), jnp.sum(grad_value, axis=0)])
    grad_qkv = jnp.concatenate(
        [grad_query, grad_key.reshape(tokens, model_width), grad_value], axis=1
    ).astype(jnp.bfloat16)
    grad_norm_in = jnp.dot(grad_qkv, qkv_back.T, preferred_element_type=jnp.float32)
    grad_gain_in = jnp.sum(grad_norm_in * normed_in, axis=0)
    grad_shift_in = jnp.sum(grad_norm_in, axis=0)
    grad_input = grad_res + norm_back(grad_norm_in, normed_in, inv_in, gain_one)
    column_parts = (
        lax.all_to_all(grad_qkv, "ctx", split_axis=1, concat_axis=0, tiled=True),
        lax.all_to_all(grad_res_bf, "ctx", split_axis=1, concat_axis=0, tiled=True),
        lax.all_to_all(grad_pre_bf, "ctx", split_axis=1, concat_axis=0, tiled=True),
        lax.all_to_all(act_ff, "ctx", split_axis=1, concat_axis=0, tiled=True),
    )
    weight_init = tuple(
        (jnp.zeros((model_width, columns.shape[1]), jnp.float32) for columns in column_parts)
    )
    pieces = (
        lax.all_gather(act_in, "ctx", axis=0, tiled=True),
        lax.all_gather(attended_bf, "ctx", axis=0, tiled=True),
        lax.all_gather(act_mid, "ctx", axis=0, tiled=True),
        lax.all_gather(upstream, "ctx", axis=0, tiled=True),
    )
    updated = []
    for total, piece, columns in zip(weight_init, pieces, column_parts):
        updated.append(jnp.dot(piece.T, columns, preferred_element_type=jnp.float32))
    grad_w_qkv, grad_w_out, grad_w_fc, grad_w_down = tuple(updated)
    vector_totals = lax.psum(
        (
            grad_gain_in,
            grad_shift_in,
            grad_qv_bias,
            grad_out_bias,
            grad_gain_mid,
            grad_shift_mid,
            grad_fc_bias,
            grad_down_bias,
        ),
        "ctx",
    )
    gain_a, shift_a, bias_qv, bias_out, gain_b, shift_b, bias_fc, bias_down = vector_totals
    summed = (
        lax.psum_scatter(grad_w_qkv, "fsdp", scatter_dimension=0, tiled=True),
        lax.psum_scatter(grad_w_out, "fsdp", scatter_dimension=0, tiled=True),
        lax.psum_scatter(grad_w_fc, "fsdp", scatter_dimension=0, tiled=True),
        lax.psum_scatter(grad_w_down, "fsdp", scatter_dimension=0, tiled=True),
        lax.psum_scatter(gain_a, "fsdp", scatter_dimension=0, tiled=True),
        lax.psum_scatter(shift_a, "fsdp", scatter_dimension=0, tiled=True),
        lax.psum_scatter(bias_qv, "fsdp", scatter_dimension=0, tiled=True),
        lax.psum_scatter(bias_out, "fsdp", scatter_dimension=0, tiled=True),
        lax.psum_scatter(gain_b, "fsdp", scatter_dimension=0, tiled=True),
        lax.psum_scatter(shift_b, "fsdp", scatter_dimension=0, tiled=True),
        lax.psum_scatter(bias_fc, "fsdp", scatter_dimension=0, tiled=True),
        lax.psum_scatter(bias_down, "fsdp", scatter_dimension=0, tiled=True),
    )
    return (
        result.reshape(1, tokens, model_width),
        grad_input.reshape(1, tokens, model_width),
        summed[4],
        summed[5],
        summed[0],
        summed[6],
        summed[1],
        summed[7],
        summed[8],
        summed[9],
        summed[2],
        summed[10],
        summed[3],
        summed[11],
    )


def solution(mesh):
    in_specs = (
        P("fsdp", "ctx", None),
        P("fsdp", "ctx", None),
        P(),
        P("fsdp"),
        P("fsdp"),
        P("fsdp", None),
        P("fsdp"),
        P("fsdp", None),
        P("fsdp"),
        P("fsdp"),
        P("fsdp"),
        P("fsdp", None),
        P("fsdp"),
        P("fsdp", None),
        P("fsdp"),
    )
    out_specs = (
        P("fsdp", "ctx", None),
        P("fsdp", "ctx", None),
        P("fsdp"),
        P("fsdp"),
        P("fsdp", "ctx"),
        P("fsdp"),
        P("fsdp", "ctx"),
        P("fsdp"),
        P("fsdp"),
        P("fsdp"),
        P("fsdp", "ctx"),
        P("fsdp"),
        P("fsdp", "ctx"),
        P("fsdp"),
    )
    return jax.shard_map(local, mesh=mesh, in_specs=in_specs, out_specs=out_specs, check_vma=False)
```

profile of v0, /device:TPU:0, one launch (start us, length us, event | category | flops | bytes accessed | tf_op | source)
XLA Modules:
  0.0 1433.2 jit_solution(6924254274625529990)
XLA Ops:
  16.3 14.2 all-gather.13.cloned.1.call-done
  30.6 6.1 fusion.39
  42.4 88.9 %all-gather.15.cloned.1.call-done = bf16[2048,17,64]{0,2,1:T(8,128)(2,1)} async-done(((bf16[128,17,64]{0,2,1:T(8,128)(2,1)}), bf16[2048,17,64]{0,2,1:T(8,128)(2,1)}) %all-gather.15.cloned.1.call-update) | async-done | bytes 4456464 | tf_op jit(solution)/shard_map/all_gather | solution.py:191
  131.2 5.1 copy.87
  136.3 88.2 %all-gather.17.cloned.1.call-done = bf16[2048,17,64]{0,2,1:T(8,128)(2,1)} async-done(((bf16[128,17,64]{0,2,1:T(8,128)(2,1)}), bf16[2048,17,64]{0,2,1:T(8,128)(2,1)}) %all-gather.17.cloned.1.call-update) | async-done | bytes 4456464 | tf_op jit(solution)/shard_map/all_gather | solution.py:192
  224.5 5.0 copy.86
  229.6 39.7 %while.40 = (s32[]{:T(128)}, f32[17,128]{1,0:T(8,128)S(1)}, f32[17,128]{1,0:T(8,128)S(1)}, f32[128,17,64]{0,2,1:T(8,128)S(1)}, s32[4]{0:T(128)S(1)}, /*index=5*/...) while((s32[]{:T(128)}, f32[17,128]{1,0:T(8,128)S(1)}, ...), condition=%wide.region_11.12_spmd, body=%wide.region_4.11_spmd.sunk | while | flops 300111232 | bytes 17405872 | solution.py:75
  232.9 6.4 conditional.4
  242.7 6.8 conditional.4
  252.8 6.7 conditional.4
  262.9 6.4 conditional.4
  276.5 9.3 multiply_convert_fusion
  285.7 7.4 fusion.85
  299.1 908.4 %while.41 = (s32[]{:T(128)}, bf16[128,17,64]{0,2,1:T(8,128)(2,1)}, bf16[128,17,64]{0,2,1:T(8,128)(2,1)}, f32[128,17,64]{0,2,1:T(8,128)S(1)}, f32[128,17,64]{0,2,...) while((s32[]{:T(128)}, bf16[128,17,64]{0,2,1:T(8,128)(2,1)}, ...), condition=%wide.region_22.23_spmd, body=%wide.region_17.22_spmd.sunk | while | flops 180936464 | bytes 18158836 | solution.py:287
  303.3 3.9 conditional.5
  312.0 50.5 %collective-permute-done = bf16[128,17,64]{0,2,1:T(8,128)(2,1)} collective-permute-done((bf16[128,17,64]{0,2,1:T(8,128)(2,1)S(1)}, bf16[128,17,64]{0,2,1:T(8,128)(2,1)}, u32[]{:S(2)}, u32[]{:S(2)}) %collective-permute-start) | collective-permute-done | bytes 278560 | tf_op jit(solution)/shard_map/while/body/eval_jaxpr/ppermute | solution.py:18
  362.5 5.3 collective-permute-done.1
  376.5 60.6 %collective-permute-done = bf16[128,17,64]{0,2,1:T(8,128)(2,1)} collective-permute-done((bf16[128,17,64]{0,2,1:T(8,128)(2,1)S(1)}, bf16[128,17,64]{0,2,1:T(8,128)(2,1)}, u32[]{:S(2)}, u32[]{:S(2)}) %collective-permute-start) | collective-permute-done | bytes 278560 | tf_op jit(solution)/shard_map/while/body/eval_jaxpr/ppermute | solution.py:18
  437.1 11.4 collective-permute-done.1
  452.5 3.9 conditional.5
  458.3 35.7 %collective-permute-done = bf16[128,17,64]{0,2,1:T(8,128)(2,1)} collective-permute-done((bf16[128,17,64]{0,2,1:T(8,128)(2,1)S(1)}, bf16[128,17,64]{0,2,1:T(8,128)(2,1)}, u32[]{:S(2)}, u32[]{:S(2)}) %collective-permute-start) | collective-permute-done | bytes 278560 | tf_op jit(solution)/shard_map/while/body/eval_jaxpr/ppermute | solution.py:18
  501.5 3.9 conditional.5
  505.7 54.2 %collective-permute-done = bf16[128,17,64]{0,2,1:T(8,128)(2,1)} collective-permute-done((bf16[128,17,64]{0,2,1:T(8,128)(2,1)S(1)}, bf16[128,17,64]{0,2,1:T(8,128)(2,1)}, u32[]{:S(2)}, u32[]{:S(2)}) %collective-permute-start) | collective-permute-done | bytes 278560 | tf_op jit(solution)/shard_map/while/body/eval_jaxpr/ppermute | solution.py:18
  567.3 3.9 conditional.5
  571.5 61.5 %collective-permute-done = bf16[128,17,64]{0,2,1:T(8,128)(2,1)} collective-permute-done((bf16[128,17,64]{0,2,1:T(8,128)(2,1)S(1)}, bf16[128,17,64]{0,2,1:T(8,128)(2,1)}, u32[]{:S(2)}, u32[]{:S(2)}) %collective-permute-start) | collective-permute-done | bytes 278560 | tf_op jit(solution)/shard_map/while/body/eval_jaxpr/ppermute | solution.py:18
  633.0 10.8 collective-permute-done.1
  647.7 3.9 conditional.5
  651.9 36.0 %collective-permute-done = bf16[128,17,64]{0,2,1:T(8,128)(2,1)} collective-permute-done((bf16[128,17,64]{0,2,1:T(8,128)(2,1)S(1)}, bf16[128,17,64]{0,2,1:T(8,128)(2,1)}, u32[]{:S(2)}, u32[]{:S(2)}) %collective-permute-start) | collective-permute-done | bytes 278560 | tf_op jit(solution)/shard_map/while/body/eval_jaxpr/ppermute | solution.py:18
  698.5 51.0 %collective-permute-done = bf16[128,17,64]{0,2,1:T(8,128)(2,1)} collective-permute-done((bf16[128,17,64]{0,2,1:T(8,128)(2,1)S(1)}, bf16[128,17,64]{0,2,1:T(8,128)(2,1)}, u32[]{:S(2)}, u32[]{:S(2)}) %collective-permute-start) | collective-permute-done | bytes 278560 | tf_op jit(solution)/shard_map/while/body/eval_jaxpr/ppermute | solution.py:18
  756.5 3.9 conditional.5
  760.7 64.0 %collective-permute-done = bf16[128,17,64]{0,2,1:T(8,128)(2,1)} collective-permute-done((bf16[128,17,64]{0,2,1:T(8,128)(2,1)S(1)}, bf16[128,17,64]{0,2,1:T(8,128)(2,1)}, u32[]{:S(2)}, u32[]{:S(2)}) %collective-permute-start) | collective-permute-done | bytes 278560 | tf_op jit(solution)/shard_map/while/body/eval_jaxpr/ppermute | solution.py:18
  824.6 8.8 collective-permute-done.1
  837.4 3.9 conditional.5
  841.5 25.8 %collective-permute-done = bf16[128,17,64]{0,2,1:T(8,128)(2,1)} collective-permute-done((bf16[128,17,64]{0,2,1:T(8,128)(2,1)S(1)}, bf16[128,17,64]{0,2,1:T(8,128)(2,1)}, u32[]{:S(2)}, u32[]{:S(2)}) %collective-permute-start) | collective-permute-done | bytes 278560 | tf_op jit(solution)/shard_map/while/body/eval_jaxpr/ppermute | solution.py:18
  874.3 3.9 conditional.5
  880.4 22.7 %collective-permute-done = bf16[128,17,64]{0,2,1:T(8,128)(2,1)} collective-permute-done((bf16[128,17,64]{0,2,1:T(8,128)(2,1)S(1)}, bf16[128,17,64]{0,2,1:T(8,128)(2,1)}, u32[]{:S(2)}, u32[]{:S(2)}) %collective-permute-start) | collective-permute-done | bytes 278560 | tf_op jit(solution)/shard_map/while/body/eval_jaxpr/ppermute | solution.py:18
  903.1 4.2 collective-permute-done.1
  911.3 3.9 conditional.5
  918.8 20.1 %collective-permute-done = bf16[128,17,64]{0,2,1:T(8,128)(2,1)} collective-permute-done((bf16[128,17,64]{0,2,1:T(8,128)(2,1)S(1)}, bf16[128,17,64]{0,2,1:T(8,128)(2,1)}, u32[]{:S(2)}, u32[]{:S(2)}) %collective-permute-start) | collective-permute-done | bytes 278560 | tf_op jit(solution)/shard_map/while/body/eval_jaxpr/ppermute | solution.py:18
  945.9 3.9 conditional.5
  953.5 7.8 collective-permute-start
  961.2 9.9 collective-permute-start.1
  971.1 37.7 %collective-permute-done = bf16[128,17,64]{0,2,1:T(8,128)(2,1)} collective-permute-done((bf16[128,17,64]{0,2,1:T(8,128)(2,1)S(1)}, bf16[128,17,64]{0,2,1:T(8,128)(2,1)}, u32[]{:S(2)}, u32[]{:S(2)}) %collective-permute-start) | collective-permute-done | bytes 278560 | tf_op jit(solution)/shard_map/while/body/eval_jaxpr/ppermute | solution.py:18
  1015.8 3.9 conditional.5
  1020.2 63.8 %collective-permute-done = bf16[128,17,64]{0,2,1:T(8,128)(2,1)} collective-permute-done((bf16[128,17,64]{0,2,1:T(8,128)(2,1)S(1)}, bf16[128,17,64]{0,2,1:T(8,128)(2,1)}, u32[]{:S(2)}, u32[]{:S(2)}) %collective-permute-start) | collective-permute-done | bytes 278560 | tf_op jit(solution)/shard_map/while/body/eval_jaxpr/ppermute | solution.py:18
  1084.0 9.0 collective-permute-done.1
  1098.6 29.8 %collective-permute-done = bf16[128,17,64]{0,2,1:T(8,128)(2,1)} collective-permute-done((bf16[128,17,64]{0,2,1:T(8,128)(2,1)S(1)}, bf16[128,17,64]{0,2,1:T(8,128)(2,1)}, u32[]{:S(2)}, u32[]{:S(2)}) %collective-permute-start) | collective-permute-done | bytes 278560 | tf_op jit(solution)/shard_map/while/body/eval_jaxpr/ppermute | solution.py:18
  1135.3 3.9 conditional.5
  1139.5 28.6 %collective-permute-done = bf16[128,17,64]{0,2,1:T(8,128)(2,1)} collective-permute-done((bf16[128,17,64]{0,2,1:T(8,128)(2,1)S(1)}, bf16[128,17,64]{0,2,1:T(8,128)(2,1)}, u32[]{:S(2)}, u32[]{:S(2)}) %collective-permute-start) | collective-permute-done | bytes 278560 | tf_op jit(solution)/shard_map/while/body/eval_jaxpr/ppermute | solution.py:18
  1177.6 27.0 %collective-permute-done = bf16[128,17,64]{0,2,1:T(8,128)(2,1)} collective-permute-done((bf16[128,17,64]{0,2,1:T(8,128)(2,1)S(1)}, bf16[128,17,64]{0,2,1:T(8,128)(2,1)}, u32[]{:S(2)}, u32[]{:S(2)}) %collective-permute-start) | collective-permute-done | bytes 278560 | tf_op jit(solution)/shard_map/while/body/eval_jaxpr/ppermute | solution.py:18
  1210.7 17.0 %all-to-all-start = ((bf16[128,16,204]{0,2,1:T(8,128)(2,1)}), bf16[128,16,204]{0,2,1:T(8,128)(2,1)}, u32[]{:S(2)}, u32[]{:S(2)}) async-start(bf16[128,16,204]{0,2,1:T(8,128)(2,1)} %convert_element_type.132), calls=%async_computation | async-start | bytes 1703936 | tf_op jit(solution)/shard_map/all_to_all | solution.py:304
  1229.2 16.6 %all-to-all-done = bf16[128,16,204]{0,2,1:T(8,128)(2,1)} async-done(((bf16[128,16,204]{0,2,1:T(8,128)(2,1)}), bf16[128,16,204]{0,2,1:T(8,128)(2,1)}, u32[]{:S(2)}, u32[]{:S(2)}) %all-to-all-start) | async-done | bytes 835616 | tf_op jit(solution)/shard_map/all_to_all | solution.py:304
  1245.7 10.2 all-to-all-start.3
  1258.7 4.9 fusion.89
  1264.3 11.4 all-to-all-done.3
  1275.7 4.8 all-to-all-start.1
  1280.6 5.3 fusion.42
  1293.8 4.4 all-to-all-start.2
  1298.5 4.5 fusion.90
  1303.3 11.3 all-to-all-done.2
  1314.6 6.3 fusion.56
  1323.6 5.7 fusion.73
  1333.6 76.0 %all-reduce.15 = (f32[544]{0:T(1024)}, f32[544]{0:T(1024)}, f32[1088]{0:T(1024)}, f32[544]{0:T(1024)}, f32[544]{0:T(1024)}, /*index=5*/f32[544]{0:T(1024)}, f32[2176]{0:T(1024)}, f32[544]{0:T(1024)}) all-reduce(f32[544]{0:T(1024)S(1)} %dynamic-slice.8, f32[544]{0:T(1024)S(1)} %dynamic-slice.10, ...), channel_id=1, replica_groups=mesh['ctx'=16,'fsdp'=2] {'ctx'}, use_global_device_ids=true, to_apply=%region_26.27 | all-reduce | flops 6528 | bytes 52224 | tf_op jit(solution)/shard_map/psum | solution.py:322
  1410.7 7.0 fusion.48
  (493 shorter events, 248.2 us)
Async XLA Ops:
  8.0 123.2 %all-gather.15.cloned.1.call-start = ((), (), s32[]{:S(2)}) async-start(), calls=%async_computation.9 | async-start | bytes 4734976 | tf_op jit(solution)/shard_map/all_gather | solution.py:191
  37.6 187.0 %all-gather.17.cloned.1.call-start = ((), (), s32[]{:S(2)}) async-start(), calls=%async_computation.10 | async-start | bytes 4734976 | tf_op jit(solution)/shard_map/all_gather | solution.py:192
  38.3 234.0 %all-gather.19.cloned.1.call-start = ((), (), s32[]{:S(2)}) async-start(), calls=%async_computation.11 | async-start | bytes 3760128 | tf_op jit(solution)/shard_map/all_gather | solution.py:109
  38.9 237.6 %all-gather.21.cloned.1.call-start = ((), (), s32[]{:S(2)}) async-start(), calls=%async_computation.12 | async-start | bytes 14204928 | tf_op jit(solution)/shard_map/all_gather | solution.py:113
  39.5 246.3 %all-gather.23.cloned.1.call-start = ((), (), s32[]{:S(2)}) async-start(), calls=%async_computation.13 | async-start | bytes 14204928 | tf_op jit(solution)/shard_map/all_gather | solution.py:115
  40.0 1218.6 %all-gather.25.cloned.1.call-start = ((), (), s32[]{:S(2)}) async-start(), calls=%async_computation.14 | async-start | bytes 4734976 | tf_op jit(solution)/shard_map/all_gather | solution.py:313
  40.8 1239.8 %all-gather.31.cloned.1.call-start = ((), (), s32[]{:S(2)}) async-start(), calls=%async_computation.17 | async-start | bytes 4734976 | tf_op jit(solution)/shard_map/all_gather | solution.py:316
  41.5 1256.9 %all-gather.27.cloned.1.call-start = ((), (), s32[]{:S(2)}) async-start(), calls=%async_computation.15 | async-start | bytes 4734976 | tf_op jit(solution)/shard_map/all_gather | solution.py:314
  270.1 1044.5 %all-gather.29.cloned.1.call-start = ((), (), s32[]{:S(2)}) async-start(), calls=%async_computation.16 | async-start | bytes 4734976 | tf_op jit(solution)/shard_map/all_gather | solution.py:315
  307.2 60.6 %collective-permute-start.2 = (f32[128,17,64]{0,2,1:T(8,128)}, f32[128,17,64]{0,2,1:T(8,128)S(1)}, u32[]{:S(2)}, u32[]{:S(2)}) collective-permute-start(f32[128,17,64]{0,2,1:T(8,128)} %get-tuple-element.1002), channel_id=1, source_target_pairs={{0,2},{2,4},{4,6},{6,8},{8,10},{10,12},{12,14},{14,16},{16,18},{18... | collective-permute-start | bytes 1671176 | tf_op jit(solution)/shard_map/while/body/eval_jaxpr/ppermute | solution.py:18
  309.0 58.8 %collective-permute-start.3 = (f32[128,17,64]{0,2,1:T(8,128)}, f32[128,17,64]{0,2,1:T(8,128)S(1)}, u32[]{:S(2)}, u32[]{:S(2)}) collective-permute-start(f32[128,17,64]{0,2,1:T(8,128)} %get-tuple-element.1003), channel_id=1, source_target_pairs={{0,2},{2,4},{4,6},{6,8},{8,10},{10,12},{12,14},{14,16},{16,18},{18... | collective-permute-start | bytes 1671176 | tf_op jit(solution)/shard_map/while/body/eval_jaxpr/ppermute | solution.py:18
  310.5 52.0 %collective-permute-start = (bf16[128,17,64]{0,2,1:T(8,128)(2,1)S(1)}, bf16[128,17,64]{0,2,1:T(8,128)(2,1)}, u32[]{:S(2)}, u32[]{:S(2)}) collective-permute-start(bf16[128,17,64]{0,2,1:T(8,128)(2,1)S(1)} %copy.128), channel_id=1, source_target_pairs={{0,2},{2,4},{4,6},{6,8},{8,10},{10,12},{12,14},{14,16},{16,18},{18... | collective-permute-start | bytes 835592 | tf_op jit(solution)/shard_map/while/body/eval_jaxpr/ppermute | solution.py:18
  312.0 55.8 %collective-permute-start.1 = (bf16[128,17,64]{0,2,1:T(8,128)(2,1)S(1)}, bf16[128,17,64]{0,2,1:T(8,128)(2,1)}, u32[]{:S(2)}, u32[]{:S(2)}) collective-permute-start(bf16[128,17,64]{0,2,1:T(8,128)(2,1)S(1)} %copy.129), channel_id=1, source_target_pairs={{0,2},{2,4},{4,6},{6,8},{8,10},{10,12},{12,14},{14,16},{16,18},{18... | collective-permute-start | bytes 835592 | tf_op jit(solution)/shard_map/while/body/eval_jaxpr/ppermute | solution.py:18
  375.7 72.8 %collective-permute-start.2 = (f32[128,17,64]{0,2,1:T(8,128)}, f32[128,17,64]{0,2,1:T(8,128)S(1)}, u32[]{:S(2)}, u32[]{:S(2)}) collective-permute-start(f32[128,17,64]{0,2,1:T(8,128)} %get-tuple-element.1002), channel_id=1, source_target_pairs={{0,2},{2,4},{4,6},{6,8},{8,10},{10,12},{12,14},{14,16},{16,18},{18... | collective-permute-start | bytes 1671176 | tf_op jit(solution)/shard_map/while/body/eval_jaxpr/ppermute | solution.py:18
  375.7 72.8 %collective-permute-start.3 = (f32[128,17,64]{0,2,1:T(8,128)}, f32[128,17,64]{0,2,1:T(8,128)S(1)}, u32[]{:S(2)}, u32[]{:S(2)}) collective-permute-start(f32[128,17,64]{0,2,1:T(8,128)} %get-tuple-element.1003), channel_id=1, source_target_pairs={{0,2},{2,4},{4,6},{6,8},{8,10},{10,12},{12,14},{14,16},{16,18},{18... | collective-permute-start | bytes 1671176 | tf_op jit(solution)/shard_map/while/body/eval_jaxpr/ppermute | solution.py:18
  375.8 61.3 %collective-permute-start = (bf16[128,17,64]{0,2,1:T(8,128)(2,1)S(1)}, bf16[128,17,64]{0,2,1:T(8,128)(2,1)}, u32[]{:S(2)}, u32[]{:S(2)}) collective-permute-start(bf16[128,17,64]{0,2,1:T(8,128)(2,1)S(1)} %copy.128), channel_id=1, source_target_pairs={{0,2},{2,4},{4,6},{6,8},{8,10},{10,12},{12,14},{14,16},{16,18},{18... | collective-permute-start | bytes 835592 | tf_op jit(solution)/shard_map/while/body/eval_jaxpr/ppermute | solution.py:18
  375.9 72.6 %collective-permute-start.1 = (bf16[128,17,64]{0,2,1:T(8,128)(2,1)S(1)}, bf16[128,17,64]{0,2,1:T(8,128)(2,1)}, u32[]{:S(2)}, u32[]{:S(2)}) collective-permute-start(bf16[128,17,64]{0,2,1:T(8,128)(2,1)S(1)} %copy.129), channel_id=1, source_target_pairs={{0,2},{2,4},{4,6},{6,8},{8,10},{10,12},{12,14},{14,16},{16,18},{18... | collective-permute-start | bytes 835592 | tf_op jit(solution)/shard_map/while/body/eval_jaxpr/ppermute | solution.py:18
  456.4 41.2 %collective-permute-start.2 = (f32[128,17,64]{0,2,1:T(8,128)}, f32[128,17,64]{0,2,1:T(8,128)S(1)}, u32[]{:S(2)}, u32[]{:S(2)}) collective-permute-start(f32[128,17,64]{0,2,1:T(8,128)} %get-tuple-element.1002), channel_id=1, source_target_pairs={{0,2},{2,4},{4,6},{6,8},{8,10},{10,12},{12,14},{14,16},{16,18},{18... | collective-permute-start | bytes 1671176 | tf_op jit(solution)/shard_map/while/body/eval_jaxpr/ppermute | solution.py:18
  456.5 41.1 %collective-permute-start.3 = (f32[128,17,64]{0,2,1:T(8,128)}, f32[128,17,64]{0,2,1:T(8,128)S(1)}, u32[]{:S(2)}, u32[]{:S(2)}) collective-permute-start(f32[128,17,64]{0,2,1:T(8,128)} %get-tuple-element.1003), channel_id=1, source_target_pairs={{0,2},{2,4},{4,6},{6,8},{8,10},{10,12},{12,14},{14,16},{16,18},{18... | collective-permute-start | bytes 1671176 | tf_op jit(solution)/shard_map/while/body/eval_jaxpr/ppermute | solution.py:18
  456.5 37.5 %collective-permute-start = (bf16[128,17,64]{0,2,1:T(8,128)(2,1)S(1)}, bf16[128,17,64]{0,2,1:T(8,128)(2,1)}, u32[]{:S(2)}, u32[]{:S(2)}) collective-permute-start(bf16[128,17,64]{0,2,1:T(8,128)(2,1)S(1)} %copy.128), channel_id=1, source_target_pairs={{0,2},{2,4},{4,6},{6,8},{8,10},{10,12},{12,14},{14,16},{16,18},{18... | collective-permute-start | bytes 835592 | tf_op jit(solution)/shard_map/while/body/eval_jaxpr/ppermute | solution.py:18
  456.6 41.0 %collective-permute-start.1 = (bf16[128,17,64]{0,2,1:T(8,128)(2,1)S(1)}, bf16[128,17,64]{0,2,1:T(8,128)(2,1)}, u32[]{:S(2)}, u32[]{:S(2)}) collective-permute-start(bf16[128,17,64]{0,2,1:T(8,128)(2,1)S(1)} %copy.129), channel_id=1, source_target_pairs={{0,2},{2,4},{4,6},{6,8},{8,10},{10,12},{12,14},{14,16},{16,18},{18... | collective-permute-start | bytes 835592 | tf_op jit(solution)/shard_map/while/body/eval_jaxpr/ppermute | solution.py:18
  505.5 57.9 %collective-permute-start.2 = (f32[128,17,64]{0,2,1:T(8,128)}, f32[128,17,64]{0,2,1:T(8,128)S(1)}, u32[]{:S(2)}, u32[]{:S(2)}) collective-permute-start(f32[128,17,64]{0,2,1:T(8,128)} %get-tuple-element.1002), channel_id=1, source_target_pairs={{0,2},{2,4},{4,6},{6,8},{8,10},{10,12},{12,14},{14,16},{16,18},{18... | collective-permute-start | bytes 1671176 | tf_op jit(solution)/shard_map/while/body/eval_jaxpr/ppermute | solution.py:18
  505.5 57.8 %collective-permute-start.3 = (f32[128,17,64]{0,2,1:T(8,128)}, f32[128,17,64]{0,2,1:T(8,128)S(1)}, u32[]{:S(2)}, u32[]{:S(2)}) collective-permute-start(f32[128,17,64]{0,2,1:T(8,128)} %get-tuple-element.1003), channel_id=1, source_target_pairs={{0,2},{2,4},{4,6},{6,8},{8,10},{10,12},{12,14},{14,16},{16,18},{18... | collective-permute-start | bytes 1671176 | tf_op jit(solution)/shard_map/while/body/eval_jaxpr/ppermute | solution.py:18
  505.6 54.4 %collective-permute-start = (bf16[128,17,64]{0,2,1:T(8,128)(2,1)S(1)}, bf16[128,17,64]{0,2,1:T(8,128)(2,1)}, u32[]{:S(2)}, u32[]{:S(2)}) collective-permute-start(bf16[128,17,64]{0,2,1:T(8,128)(2,1)S(1)} %copy.128), channel_id=1, source_target_pairs={{0,2},{2,4},{4,6},{6,8},{8,10},{10,12},{12,14},{14,16},{16,18},{18... | collective-permute-start | bytes 835592 | tf_op jit(solution)/shard_map/while/body/eval_jaxpr/ppermute | solution.py:18
  505.6 57.7 %collective-permute-start.1 = (bf16[128,17,64]{0,2,1:T(8,128)(2,1)S(1)}, bf16[128,17,64]{0,2,1:T(8,128)(2,1)}, u32[]{:S(2)}, u32[]{:S(2)}) collective-permute-start(bf16[128,17,64]{0,2,1:T(8,128)(2,1)S(1)} %copy.129), channel_id=1, source_target_pairs={{0,2},{2,4},{4,6},{6,8},{8,10},{10,12},{12,14},{14,16},{16,18},{18... | collective-permute-start | bytes 835592 | tf_op jit(solution)/shard_map/while/body/eval_jaxpr/ppermute | solution.py:18
  571.2 72.5 %collective-permute-start.2 = (f32[128,17,64]{0,2,1:T(8,128)}, f32[128,17,64]{0,2,1:T(8,128)S(1)}, u32[]{:S(2)}, u32[]{:S(2)}) collective-permute-start(f32[128,17,64]{0,2,1:T(8,128)} %get-tuple-element.1002), channel_id=1, source_target_pairs={{0,2},{2,4},{4,6},{6,8},{8,10},{10,12},{12,14},{14,16},{16,18},{18... | collective-permute-start | bytes 1671176 | tf_op jit(solution)/shard_map/while/body/eval_jaxpr/ppermute | solution.py:18
  571.3 72.5 %collective-permute-start.3 = (f32[128,17,64]{0,2,1:T(8,128)}, f32[128,17,64]{0,2,1:T(8,128)S(1)}, u32[]{:S(2)}, u32[]{:S(2)}) collective-permute-start(f32[128,17,64]{0,2,1:T(8,128)} %get-tuple-element.1003), channel_id=1, source_target_pairs={{0,2},{2,4},{4,6},{6,8},{8,10},{10,12},{12,14},{14,16},{16,18},{18... | collective-permute-start | bytes 1671176 | tf_op jit(solution)/shard_map/while/body/eval_jaxpr/ppermute | solution.py:18
  571.4 61.6 %collective-permute-start = (bf16[128,17,64]{0,2,1:T(8,128)(2,1)S(1)}, bf16[128,17,64]{0,2,1:T(8,128)(2,1)}, u32[]{:S(2)}, u32[]{:S(2)}) collective-permute-start(bf16[128,17,64]{0,2,1:T(8,128)(2,1)S(1)} %copy.128), channel_id=1, source_target_pairs={{0,2},{2,4},{4,6},{6,8},{8,10},{10,12},{12,14},{14,16},{16,18},{18... | collective-permute-start | bytes 835592 | tf_op jit(solution)/shard_map/while/body/eval_jaxpr/ppermute | solution.py:18
  571.4 72.4 %collective-permute-start.1 = (bf16[128,17,64]{0,2,1:T(8,128)(2,1)S(1)}, bf16[128,17,64]{0,2,1:T(8,128)(2,1)}, u32[]{:S(2)}, u32[]{:S(2)}) collective-permute-start(bf16[128,17,64]{0,2,1:T(8,128)(2,1)S(1)} %copy.129), channel_id=1, source_target_pairs={{0,2},{2,4},{4,6},{6,8},{8,10},{10,12},{12,14},{14,16},{16,18},{18... | collective-permute-start | bytes 835592 | tf_op jit(solution)/shard_map/while/body/eval_jaxpr/ppermute | solution.py:18
  651.7 39.3 %collective-permute-start.2 = (f32[128,17,64]{0,2,1:T(8,128)}, f32[128,17,64]{0,2,1:T(8,128)S(1)}, u32[]{:S(2)}, u32[]{:S(2)}) collective-permute-start(f32[128,17,64]{0,2,1:T(8,128)} %get-tuple-element.1002), channel_id=1, source_target_pairs={{0,2},{2,4},{4,6},{6,8},{8,10},{10,12},{12,14},{14,16},{16,18},{18... | collective-permute-start | bytes 1671176 | tf_op jit(solution)/shard_map/while/body/eval_jaxpr/ppermute | solution.py:18
  651.7 39.2 %collective-permute-start.3 = (f32[128,17,64]{0,2,1:T(8,128)}, f32[128,17,64]{0,2,1:T(8,128)S(1)}, u32[]{:S(2)}, u32[]{:S(2)}) collective-permute-start(f32[128,17,64]{0,2,1:T(8,128)} %get-tuple-element.1003), channel_id=1, source_target_pairs={{0,2},{2,4},{4,6},{6,8},{8,10},{10,12},{12,14},{14,16},{16,18},{18... | collective-permute-start | bytes 1671176 | tf_op jit(solution)/shard_map/while/body/eval_jaxpr/ppermute | solution.py:18
  651.8 36.2 %collective-permute-start = (bf16[128,17,64]{0,2,1:T(8,128)(2,1)S(1)}, bf16[128,17,64]{0,2,1:T(8,128)(2,1)}, u32[]{:S(2)}, u32[]{:S(2)}) collective-permute-start(bf16[128,17,64]{0,2,1:T(8,128)(2,1)S(1)} %copy.128), channel_id=1, source_target_pairs={{0,2},{2,4},{4,6},{6,8},{8,10},{10,12},{12,14},{14,16},{16,18},{18... | collective-permute-start | bytes 835592 | tf_op jit(solution)/shard_map/while/body/eval_jaxpr/ppermute | solution.py:18
  651.9 39.1 %collective-permute-start.1 = (bf16[128,17,64]{0,2,1:T(8,128)(2,1)S(1)}, bf16[128,17,64]{0,2,1:T(8,128)(2,1)}, u32[]{:S(2)}, u32[]{:S(2)}) collective-permute-start(bf16[128,17,64]{0,2,1:T(8,128)(2,1)S(1)} %copy.129), channel_id=1, source_target_pairs={{0,2},{2,4},{4,6},{6,8},{8,10},{10,12},{12,14},{14,16},{16,18},{18... | collective-permute-start | bytes 835592 | tf_op jit(solution)/shard_map/while/body/eval_jaxpr/ppermute | solution.py:18
  696.5 56.0 %collective-permute-start.2 = (f32[128,17,64]{0,2,1:T(8,128)}, f32[128,17,64]{0,2,1:T(8,128)S(1)}, u32[]{:S(2)}, u32[]{:S(2)}) collective-permute-start(f32[128,17,64]{0,2,1:T(8,128)} %get-tuple-element.1002), channel_id=1, source_target_pairs={{0,2},{2,4},{4,6},{6,8},{8,10},{10,12},{12,14},{14,16},{16,18},{18... | collective-permute-start | bytes 1671176 | tf_op jit(solution)/shard_map/while/body/eval_jaxpr/ppermute | solution.py:18
  698.3 54.2 %collective-permute-start.3 = (f32[128,17,64]{0,2,1:T(8,128)}, f32[128,17,64]{0,2,1:T(8,128)S(1)}, u32[]{:S(2)}, u32[]{:S(2)}) collective-permute-start(f32[128,17,64]{0,2,1:T(8,128)} %get-tuple-element.1003), channel_id=1, source_target_pairs={{0,2},{2,4},{4,6},{6,8},{8,10},{10,12},{12,14},{14,16},{16,18},{18... | collective-permute-start | bytes 1671176 | tf_op jit(solution)/shard_map/while/body/eval_jaxpr/ppermute | solution.py:18
  698.4 51.1 %collective-permute-start = (bf16[128,17,64]{0,2,1:T(8,128)(2,1)S(1)}, bf16[128,17,64]{0,2,1:T(8,128)(2,1)}, u32[]{:S(2)}, u32[]{:S(2)}) collective-permute-start(bf16[128,17,64]{0,2,1:T(8,128)(2,1)S(1)} %copy.128), channel_id=1, source_target_pairs={{0,2},{2,4},{4,6},{6,8},{8,10},{10,12},{12,14},{14,16},{16,18},{18... | collective-permute-start | bytes 835592 | tf_op jit(solution)/shard_map/while/body/eval_jaxpr/ppermute | solution.py:18
  698.5 54.0 %collective-permute-start.1 = (bf16[128,17,64]{0,2,1:T(8,128)(2,1)S(1)}, bf16[128,17,64]{0,2,1:T(8,128)(2,1)}, u32[]{:S(2)}, u32[]{:S(2)}) collective-permute-start(bf16[128,17,64]{0,2,1:T(8,128)(2,1)S(1)} %copy.129), channel_id=1, source_target_pairs={{0,2},{2,4},{4,6},{6,8},{8,10},{10,12},{12,14},{14,16},{16,18},{18... | collective-permute-start | bytes 835592 | tf_op jit(solution)/shard_map/while/body/eval_jaxpr/ppermute | solution.py:18
  760.4 73.0 %collective-permute-start.2 = (f32[128,17,64]{0,2,1:T(8,128)}, f32[128,17,64]{0,2,1:T(8,128)S(1)}, u32[]{:S(2)}, u32[]{:S(2)}) collective-permute-start(f32[128,17,64]{0,2,1:T(8,128)} %get-tuple-element.1002), channel_id=1, source_target_pairs={{0,2},{2,4},{4,6},{6,8},{8,10},{10,12},{12,14},{14,16},{16,18},{18... | collective-permute-start | bytes 1671176 | tf_op jit(solution)/shard_map/while/body/eval_jaxpr/ppermute | solution.py:18
  760.5 72.9 %collective-permute-start.3 = (f32[128,17,64]{0,2,1:T(8,128)}, f32[128,17,64]{0,2,1:T(8,128)S(1)}, u32[]{:S(2)}, u32[]{:S(2)}) collective-permute-start(f32[128,17,64]{0,2,1:T(8,128)} %get-tuple-element.1003), channel_id=1, source_target_pairs={{0,2},{2,4},{4,6},{6,8},{8,10},{10,12},{12,14},{14,16},{16,18},{18... | collective-permute-start | bytes 1671176 | tf_op jit(solution)/shard_map/while/body/eval_jaxpr/ppermute | solution.py:18
  760.5 64.1 %collective-permute-start = (bf16[128,17,64]{0,2,1:T(8,128)(2,1)S(1)}, bf16[128,17,64]{0,2,1:T(8,128)(2,1)}, u32[]{:S(2)}, u32[]{:S(2)}) collective-permute-start(bf16[128,17,64]{0,2,1:T(8,128)(2,1)S(1)} %copy.128), channel_id=1, source_target_pairs={{0,2},{2,4},{4,6},{6,8},{8,10},{10,12},{12,14},{14,16},{16,18},{18... | collective-permute-start | bytes 835592 | tf_op jit(solution)/shard_map/while/body/eval_jaxpr/ppermute | solution.py:18
  760.6 72.8 %collective-permute-start.1 = (bf16[128,17,64]{0,2,1:T(8,128)(2,1)S(1)}, bf16[128,17,64]{0,2,1:T(8,128)(2,1)}, u32[]{:S(2)}, u32[]{:S(2)}) collective-permute-start(bf16[128,17,64]{0,2,1:T(8,128)(2,1)S(1)} %copy.129), channel_id=1, source_target_pairs={{0,2},{2,4},{4,6},{6,8},{8,10},{10,12},{12,14},{14,16},{16,18},{18... | collective-permute-start | bytes 835592 | tf_op jit(solution)/shard_map/while/body/eval_jaxpr/ppermute | solution.py:18
  949.8 62.0 %collective-permute-start.2 = (f32[128,17,64]{0,2,1:T(8,128)}, f32[128,17,64]{0,2,1:T(8,128)S(1)}, u32[]{:S(2)}, u32[]{:S(2)}) collective-permute-start(f32[128,17,64]{0,2,1:T(8,128)} %get-tuple-element.1002), channel_id=1, source_target_pairs={{0,2},{2,4},{4,6},{6,8},{8,10},{10,12},{12,14},{14,16},{16,18},{18... | collective-permute-start | bytes 1671176 | tf_op jit(solution)/shard_map/while/body/eval_jaxpr/ppermute | solution.py:18
  950.0 61.8 %collective-permute-start.3 = (f32[128,17,64]{0,2,1:T(8,128)}, f32[128,17,64]{0,2,1:T(8,128)S(1)}, u32[]{:S(2)}, u32[]{:S(2)}) collective-permute-start(f32[128,17,64]{0,2,1:T(8,128)} %get-tuple-element.1003), channel_id=1, source_target_pairs={{0,2},{2,4},{4,6},{6,8},{8,10},{10,12},{12,14},{14,16},{16,18},{18... | collective-permute-start | bytes 1671176 | tf_op jit(solution)/shard_map/while/body/eval_jaxpr/ppermute | solution.py:18
  953.5 55.4 %collective-permute-start = (bf16[128,17,64]{0,2,1:T(8,128)(2,1)S(1)}, bf16[128,17,64]{0,2,1:T(8,128)(2,1)}, u32[]{:S(2)}, u32[]{:S(2)}) collective-permute-start(bf16[128,17,64]{0,2,1:T(8,128)(2,1)S(1)} %copy.128), channel_id=1, source_target_pairs={{0,2},{2,4},{4,6},{6,8},{8,10},{10,12},{12,14},{14,16},{16,18},{18... | collective-permute-start | bytes 835592 | tf_op jit(solution)/shard_map/while/body/eval_jaxpr/ppermute | solution.py:18
  961.2 50.6 %collective-permute-start.1 = (bf16[128,17,64]{0,2,1:T(8,128)(2,1)S(1)}, bf16[128,17,64]{0,2,1:T(8,128)(2,1)}, u32[]{:S(2)}, u32[]{:S(2)}) collective-permute-start(bf16[128,17,64]{0,2,1:T(8,128)(2,1)S(1)} %copy.129), channel_id=1, source_target_pairs={{0,2},{2,4},{4,6},{6,8},{8,10},{10,12},{12,14},{14,16},{16,18},{18... | collective-permute-start | bytes 835592 | tf_op jit(solution)/shard_map/while/body/eval_jaxpr/ppermute | solution.py:18
  1019.7 73.3 %collective-permute-start.2 = (f32[128,17,64]{0,2,1:T(8,128)}, f32[128,17,64]{0,2,1:T(8,128)S(1)}, u32[]{:S(2)}, u32[]{:S(2)}) collective-permute-start(f32[128,17,64]{0,2,1:T(8,128)} %get-tuple-element.1002), channel_id=1, source_target_pairs={{0,2},{2,4},{4,6},{6,8},{8,10},{10,12},{12,14},{14,16},{16,18},{18... | collective-permute-start | bytes 1671176 | tf_op jit(solution)/shard_map/while/body/eval_jaxpr/ppermute | solution.py:18
  1019.7 73.2 %collective-permute-start.3 = (f32[128,17,64]{0,2,1:T(8,128)}, f32[128,17,64]{0,2,1:T(8,128)S(1)}, u32[]{:S(2)}, u32[]{:S(2)}) collective-permute-start(f32[128,17,64]{0,2,1:T(8,128)} %get-tuple-element.1003), channel_id=1, source_target_pairs={{0,2},{2,4},{4,6},{6,8},{8,10},{10,12},{12,14},{14,16},{16,18},{18... | collective-permute-start | bytes 1671176 | tf_op jit(solution)/shard_map/while/body/eval_jaxpr/ppermute | solution.py:18
  1019.8 64.2 %collective-permute-start = (bf16[128,17,64]{0,2,1:T(8,128)(2,1)S(1)}, bf16[128,17,64]{0,2,1:T(8,128)(2,1)}, u32[]{:S(2)}, u32[]{:S(2)}) collective-permute-start(bf16[128,17,64]{0,2,1:T(8,128)(2,1)S(1)} %copy.128), channel_id=1, source_target_pairs={{0,2},{2,4},{4,6},{6,8},{8,10},{10,12},{12,14},{14,16},{16,18},{18... | collective-permute-start | bytes 835592 | tf_op jit(solution)/shard_map/while/body/eval_jaxpr/ppermute | solution.py:18
  1019.9 73.1 %collective-permute-start.1 = (bf16[128,17,64]{0,2,1:T(8,128)(2,1)S(1)}, bf16[128,17,64]{0,2,1:T(8,128)(2,1)}, u32[]{:S(2)}, u32[]{:S(2)}) collective-permute-start(bf16[128,17,64]{0,2,1:T(8,128)(2,1)S(1)} %copy.129), channel_id=1, source_target_pairs={{0,2},{2,4},{4,6},{6,8},{8,10},{10,12},{12,14},{14,16},{16,18},{18... | collective-permute-start | bytes 835592 | tf_op jit(solution)/shard_map/while/body/eval_jaxpr/ppermute | solution.py:18
  1098.5 32.9 %collective-permute-start.2 = (f32[128,17,64]{0,2,1:T(8,128)}, f32[128,17,64]{0,2,1:T(8,128)S(1)}, u32[]{:S(2)}, u32[]{:S(2)}) collective-permute-start(f32[128,17,64]{0,2,1:T(8,128)} %get-tuple-element.1002), channel_id=1, source_target_pairs={{0,2},{2,4},{4,6},{6,8},{8,10},{10,12},{12,14},{14,16},{16,18},{18... | collective-permute-start | bytes 1671176 | tf_op jit(solution)/shard_map/while/body/eval_jaxpr/ppermute | solution.py:18
  1098.5 32.9 %collective-permute-start.3 = (f32[128,17,64]{0,2,1:T(8,128)}, f32[128,17,64]{0,2,1:T(8,128)S(1)}, u32[]{:S(2)}, u32[]{:S(2)}) collective-permute-start(f32[128,17,64]{0,2,1:T(8,128)} %get-tuple-element.1003), channel_id=1, source_target_pairs={{0,2},{2,4},{4,6},{6,8},{8,10},{10,12},{12,14},{14,16},{16,18},{18... | collective-permute-start | bytes 1671176 | tf_op jit(solution)/shard_map/while/body/eval_jaxpr/ppermute | solution.py:18
  1098.5 32.8 %collective-permute-start.1 = (bf16[128,17,64]{0,2,1:T(8,128)(2,1)S(1)}, bf16[128,17,64]{0,2,1:T(8,128)(2,1)}, u32[]{:S(2)}, u32[]{:S(2)}) collective-permute-start(bf16[128,17,64]{0,2,1:T(8,128)(2,1)S(1)} %copy.129), channel_id=1, source_target_pairs={{0,2},{2,4},{4,6},{6,8},{8,10},{10,12},{12,14},{14,16},{16,18},{18... | collective-permute-start | bytes 835592 | tf_op jit(solution)/shard_map/while/body/eval_jaxpr/ppermute | solution.py:18
  1139.3 31.9 %collective-permute-start.2 = (f32[128,17,64]{0,2,1:T(8,128)}, f32[128,17,64]{0,2,1:T(8,128)S(1)}, u32[]{:S(2)}, u32[]{:S(2)}) collective-permute-start(f32[128,17,64]{0,2,1:T(8,128)} %get-tuple-element.1002), channel_id=1, source_target_pairs={{0,2},{2,4},{4,6},{6,8},{8,10},{10,12},{12,14},{14,16},{16,18},{18... | collective-permute-start | bytes 1671176 | tf_op jit(solution)/shard_map/while/body/eval_jaxpr/ppermute | solution.py:18
  1139.3 31.8 %collective-permute-start.3 = (f32[128,17,64]{0,2,1:T(8,128)}, f32[128,17,64]{0,2,1:T(8,128)S(1)}, u32[]{:S(2)}, u32[]{:S(2)}) collective-permute-start(f32[128,17,64]{0,2,1:T(8,128)} %get-tuple-element.1003), channel_id=1, source_target_pairs={{0,2},{2,4},{4,6},{6,8},{8,10},{10,12},{12,14},{14,16},{16,18},{18... | collective-permute-start | bytes 1671176 | tf_op jit(solution)/shard_map/while/body/eval_jaxpr/ppermute | solution.py:18
  1139.5 31.7 %collective-permute-start.1 = (bf16[128,17,64]{0,2,1:T(8,128)(2,1)S(1)}, bf16[128,17,64]{0,2,1:T(8,128)(2,1)}, u32[]{:S(2)}, u32[]{:S(2)}) collective-permute-start(bf16[128,17,64]{0,2,1:T(8,128)(2,1)S(1)} %copy.129), channel_id=1, source_target_pairs={{0,2},{2,4},{4,6},{6,8},{8,10},{10,12},{12,14},{14,16},{16,18},{18... | collective-permute-start | bytes 835592 | tf_op jit(solution)/shard_map/while/body/eval_jaxpr/ppermute | solution.py:18
  1176.7 30.8 %collective-permute-start.2 = (f32[128,17,64]{0,2,1:T(8,128)}, f32[128,17,64]{0,2,1:T(8,128)S(1)}, u32[]{:S(2)}, u32[]{:S(2)}) collective-permute-start(f32[128,17,64]{0,2,1:T(8,128)} %get-tuple-element.1002), channel_id=1, source_target_pairs={{0,2},{2,4},{4,6},{6,8},{8,10},{10,12},{12,14},{14,16},{16,18},{18... | collective-permute-start | bytes 1671176 | tf_op jit(solution)/shard_map/while/body/eval_jaxpr/ppermute | solution.py:18
  1176.7 30.8 %collective-permute-start.3 = (f32[128,17,64]{0,2,1:T(8,128)}, f32[128,17,64]{0,2,1:T(8,128)S(1)}, u32[]{:S(2)}, u32[]{:S(2)}) collective-permute-start(f32[128,17,64]{0,2,1:T(8,128)} %get-tuple-element.1003), channel_id=1, source_target_pairs={{0,2},{2,4},{4,6},{6,8},{8,10},{10,12},{12,14},{14,16},{16,18},{18... | collective-permute-start | bytes 1671176 | tf_op jit(solution)/shard_map/while/body/eval_jaxpr/ppermute | solution.py:18
  1176.7 30.8 %collective-permute-start.1 = (bf16[128,17,64]{0,2,1:T(8,128)(2,1)S(1)}, bf16[128,17,64]{0,2,1:T(8,128)(2,1)}, u32[]{:S(2)}, u32[]{:S(2)}) collective-permute-start(bf16[128,17,64]{0,2,1:T(8,128)(2,1)S(1)} %copy.129), channel_id=1, source_target_pairs={{0,2},{2,4},{4,6},{6,8},{8,10},{10,12},{12,14},{14,16},{16,18},{18... | collective-permute-start | bytes 835592 | tf_op jit(solution)/shard_map/while/body/eval_jaxpr/ppermute | solution.py:18
  1210.7 35.0 %all-to-all-start = ((bf16[128,16,204]{0,2,1:T(8,128)(2,1)}), bf16[128,16,204]{0,2,1:T(8,128)(2,1)}, u32[]{:S(2)}, u32[]{:S(2)}) async-start(bf16[128,16,204]{0,2,1:T(8,128)(2,1)} %convert_element_type.132), calls=%async_computation | async-start | bytes 1703936 | tf_op jit(solution)/shard_map/all_to_all | solution.py:304
  1245.7 30.0 %all-to-all-start.3 = ((bf16[128,16,272]{0,2,1:T(8,128)(2,1)}), bf16[128,16,272]{0,2,1:T(8,128)(2,1)}, u32[]{:S(2)}, u32[]{:S(2)}) async-start(bf16[128,16,272]{0,2,1:T(8,128)(2,1)} %bitcast.203), calls=%async_computation.3 | async-start | bytes 2228224 | tf_op jit(solution)/shard_map/all_to_all | solution.py:307
  1255.9 161.8 %reduce-scatter.13.cloned.1.call-start = ((), (), s32[]{:S(2)}) async-start(), calls=%async_computation.18 | async-start | bytes 1671168
  1280.5 139.3 %reduce-scatter.19.cloned.1.call-start = ((), (), s32[]{:S(2)}) async-start(), calls=%async_computation.21 | async-start | bytes 2506752
  1298.2 123.9 %reduce-scatter.15.cloned.1.call-start = ((), (), s32[]{:S(2)}) async-start(), calls=%async_computation.19 | async-start | bytes 835584
  1303.0 120.9 %reduce-scatter.17.cloned.1.call-start = ((), (), s32[]{:S(2)}) async-start(), calls=%async_computation.20 | async-start | bytes 2506752
  (41 other events, 709.1 us)
Sparse Core Ops, SparseCore 0:
  9.7 20.8 all-gather.12
  37.7 93.5 all-gather.14
  134.0 90.5 all-gather.16
  225.9 9.3 all-gather.18
  236.8 23.0 all-gather.20
  261.3 23.0 all-gather.22
  287.6 148.1 all-gather.24
  438.5 191.3 all-gather.30
  633.2 189.1 all-gather.26
  824.9 252.6 all-gather.28
  1263.7 9.8 reduce-scatter.12
  1289.0 10.4 reduce-scatter.18
  1303.1 9.2 reduce-scatter.14
  1321.1 8.8 reduce-scatter.16
where the time goes:
time: 1460 us; the launch traced here: 1430 us
  waiting for transfers between devices  987 us (68%)
  matrix products  134 us (9%)
  blocking collectives  85.4 us (6%)
  starting transfers between devices  76.6 us (5%)
  local copies, waits for them, and re-layouts  74.7 us (5%)
  loops' own time  30.1 us (2%)
  other arithmetic  27 us (2%)
  between operations  18.2 us (1%)
    ppermute x64, waiting for transfers between devices, from_behind(): lax.ppermute(shard, axis, [(i, (i + by) % size) for i in range(size)])  749 us
    all_gather x1, waiting for transfers between devices, local(): lax.all_gather(keys_own, 'ctx', axis=0, tiled=True)  88.9 us
    all_gather x1, waiting for transfers between devices, local(): lax.all_gather(values_own, 'ctx', axis=0, tiled=True)  88.2 us
    psum x1, blocking collectives, local(): lax.psum((grad_gain_in, grad_shift_in, grad_qv_bias, grad_out_bias, grad_...  76 us
    ppermute x64, starting transfers between devices, from_behind(): lax.ppermute(shard, axis, [(i, (i + by) % size) for i in range(size)])  39.4 us
    another operation x36, local copies, waits for them, and re-layouts  30.8 us
  transfers between devices with their start and end apart: 82, of which 39 were waited for; matrix products, arithmetic and copies ran while one was open for 16% of the time, Pallas kernels for 0%

commit v1 on v0

v1 whole, which is shorter than its diff:
```python
import functools
import math

import jax
import jax.numpy as jnp
from jax import lax
from jax.experimental import pallas as pl
from jax.experimental.pallas import tpu as pltpu
from jax.sharding import PartitionSpec as P

HEAD_DIM = 64


epsilon = 1e-05
gelu_scale = 0.7978845608028654
gelu_cubic = 0.044715


def layer_norm(inputs, gain_vec, shift_vec):
    average = jnp.mean(inputs, axis=-1, keepdims=True)
    centred = inputs - average
    variance = jnp.mean(centred * centred, axis=-1, keepdims=True)
    inv_std = lax.rsqrt(variance + epsilon)
    normed = centred * inv_std
    return (normed * gain_vec + shift_vec, normed, inv_std)


def norm_back(upstream, normed, inv_std, gain_vec):
    scaled = upstream * gain_vec
    mean_scaled = jnp.mean(scaled, axis=-1, keepdims=True)
    mean_cross = jnp.mean(scaled * normed, axis=-1, keepdims=True)
    return inv_std * (scaled - mean_scaled - normed * mean_cross)


def gelu_parts(pre_act):
    inner = gelu_scale * (pre_act + gelu_cubic * pre_act * pre_act * pre_act)
    tangent = jnp.tanh(inner)
    value_act = 0.5 * pre_act * (1.0 + tangent)
    slope = 0.5 * (1.0 + tangent) + 0.5 * pre_act * (1.0 - tangent * tangent) * gelu_scale * (
        1.0 + 3.0 * gelu_cubic * pre_act * pre_act
    )
    return (value_act, slope)


def block_positions(block_order, first_row, row_count, half_block):
    row_ids = first_row + jnp.arange(row_count, dtype=jnp.int32)
    block_ids = row_ids // half_block
    table_ids = jnp.arange(block_order.shape[0], dtype=jnp.int32)
    one_hot = (block_ids[:, None] == table_ids[None, :]).astype(jnp.int32)
    return jnp.sum(one_hot * block_order[None, :], axis=1) * half_block + row_ids % half_block


def attend_kernel(factor, q_ref, k_ref, v_ref, qpos_ref, kpos_ref, o_ref, lse_ref):
    scores = (
        lax.dot_general(
            q_ref[0], k_ref[0], (((1,), (1,)), ((), ())), preferred_element_type=jnp.float32
        )
        * factor
    )
    allowed = kpos_ref[...] <= qpos_ref[...]
    scores = jnp.where(allowed, scores, -1e30)
    row_max = jnp.max(scores, axis=1, keepdims=True)
    weights = jnp.exp(scores - row_max)
    total = jnp.sum(weights, axis=1, keepdims=True)
    summed = jnp.dot(weights.astype(jnp.bfloat16), v_ref[0], preferred_element_type=jnp.float32)
    o_ref[0] = summed / total
    lse_ref[0] = row_max + jnp.log(total)


def attend_back_kernel(
    factor, q_ref, k_ref, v_ref, do_ref, o_ref, lse_ref, qpos_ref, kpos_ref, dq_ref, dk_ref, dv_ref
):
    rows_q = q_ref[0]
    rows_k = k_ref[0]
    rows_do = do_ref[0]
    contract_last = (((1,), (1,)), ((), ()))
    contract_first = (((0,), (0,)), ((), ()))
    scores = (
        lax.dot_general(rows_q, rows_k, contract_last, preferred_element_type=jnp.float32) * factor
    )
    allowed = kpos_ref[...] <= qpos_ref[...]
    weights = jnp.exp(jnp.where(allowed, scores - lse_ref[0], -1e30))
    delta = jnp.sum(rows_do.astype(jnp.float32) * o_ref[0], axis=1, keepdims=True)
    grad_weights = lax.dot_general(
        rows_do, v_ref[0], contract_last, preferred_element_type=jnp.float32
    )
    grad_scores = (weights * (grad_weights - delta)).astype(jnp.bfloat16)
    dq_ref[0] = jnp.dot(grad_scores, rows_k, preferred_element_type=jnp.float32) * factor
    part_k = (
        lax.dot_general(grad_scores, rows_q, contract_first, preferred_element_type=jnp.float32)
        * factor
    )
    part_v = lax.dot_general(
        weights.astype(jnp.bfloat16), rows_do, contract_first, preferred_element_type=jnp.float32
    )

    @pl.when(pl.program_id(1) == 0)
    def _():
        dk_ref[0] = part_k
        dv_ref[0] = part_v

    @pl.when(pl.program_id(1) > 0)
    def _():
        dk_ref[0] += part_k
        dv_ref[0] += part_v


def attention_specs(q_block, key_count):
    row = pl.BlockSpec((1, q_block, HEAD_DIM), lambda h, i: (h, i, 0))
    stat = pl.BlockSpec((1, q_block, 1), lambda h, i: (h, i, 0))
    key = pl.BlockSpec((1, key_count, HEAD_DIM), lambda h, i: (h, 0, 0))
    qpos = pl.BlockSpec((q_block, 1), lambda h, i: (i, 0))
    kpos = pl.BlockSpec((1, key_count), lambda h, i: (0, 0))
    return row, stat, key, qpos, kpos


def attend(q, k, v, qpos, kpos, factor):
    heads, rows, _ = q.shape
    key_count = k.shape[1]
    q_block = min(rows, 256)
    row, stat, key, qspec, kspec = attention_specs(q_block, key_count)
    return pl.pallas_call(
        functools.partial(attend_kernel, factor),
        grid=(heads, rows // q_block),
        in_specs=[row, key, key, qspec, kspec],
        out_specs=[row, stat],
        out_shape=[
            jax.ShapeDtypeStruct((heads, rows, HEAD_DIM), jnp.float32),
            jax.ShapeDtypeStruct((heads, rows, 1), jnp.float32),
        ],
        compiler_params=pltpu.CompilerParams(vmem_limit_bytes=48 * 1024 * 1024),
        cost_estimate=pl.CostEstimate(
            flops=4 * heads * rows * key_count * HEAD_DIM,
            bytes_accessed=heads * (rows + key_count) * HEAD_DIM * 6,
            transcendentals=heads * rows * key_count,
        ),
    )(q, k, v, qpos[:, None], kpos[None, :])


def attend_back(q, k, v, do, o, lse, qpos, kpos, factor):
    heads, rows, _ = q.shape
    key_count = k.shape[1]
    q_block = min(rows, 256)
    row, stat, key, qspec, kspec = attention_specs(q_block, key_count)
    return pl.pallas_call(
        functools.partial(attend_back_kernel, factor),
        grid=(heads, rows // q_block),
        in_specs=[row, key, key, row, row, stat, qspec, kspec],
        out_specs=[row, key, key],
        out_shape=[
            jax.ShapeDtypeStruct((heads, rows, HEAD_DIM), jnp.float32),
            jax.ShapeDtypeStruct((heads, key_count, HEAD_DIM), jnp.float32),
            jax.ShapeDtypeStruct((heads, key_count, HEAD_DIM), jnp.float32),
        ],
        compiler_params=pltpu.CompilerParams(vmem_limit_bytes=56 * 1024 * 1024),
        cost_estimate=pl.CostEstimate(
            flops=10 * heads * rows * key_count * HEAD_DIM,
            bytes_accessed=heads * (rows + key_count) * HEAD_DIM * 14,
            transcendentals=heads * rows * key_count,
        ),
    )(q, k, v, do, o, lse, qpos[:, None], kpos[None, :])


def to_heads(flat):
    return jnp.transpose(flat.reshape(flat.shape[0], -1, HEAD_DIM), (1, 0, 2))


def from_heads(stacked):
    return jnp.transpose(stacked, (1, 0, 2)).reshape(stacked.shape[1], -1)


def spread(flat, count):
    return jnp.transpose(flat.reshape(flat.shape[0], count, -1), (1, 0, 2))


def unspread(stacked):
    return jnp.transpose(stacked, (1, 0, 2)).reshape(stacked.shape[1], -1)


def exchange(stacked):
    return lax.all_to_all(stacked, "ctx", split_axis=0, concat_axis=0, tiled=True)


def local(
    block_input,
    cotangent,
    block_order,
    gain_in,
    shift_in,
    w_qkv,
    qv_bias,
    w_out,
    out_bias,
    gain_mid,
    shift_mid,
    w_fc,
    fc_bias,
    w_down,
    down_bias,
):
    tokens = block_input.shape[1]
    model_width = block_input.shape[2]
    head_count = model_width // HEAD_DIM
    half_block = tokens // 2
    factor = 1.0 / math.sqrt(HEAD_DIM)
    cycle_count = lax.axis_size("ctx")
    gathered = (
        lax.all_gather(gain_in, "fsdp", axis=0, tiled=True),
        lax.all_gather(shift_in, "fsdp", axis=0, tiled=True),
        lax.all_gather(w_qkv, "fsdp", axis=0, tiled=True),
        lax.all_gather(qv_bias, "fsdp", axis=0, tiled=True),
        lax.all_gather(w_out, "fsdp", axis=0, tiled=True),
        lax.all_gather(out_bias, "fsdp", axis=0, tiled=True),
        lax.all_gather(gain_mid, "fsdp", axis=0, tiled=True),
        lax.all_gather(shift_mid, "fsdp", axis=0, tiled=True),
        lax.all_gather(w_fc, "fsdp", axis=0, tiled=True),
        lax.all_gather(fc_bias, "fsdp", axis=0, tiled=True),
        lax.all_gather(w_down, "fsdp", axis=0, tiled=True),
        lax.all_gather(down_bias, "fsdp", axis=0, tiled=True),
    )
    (
        gain_in_full,
        shift_in_full,
        qkv_full,
        qv_full,
        out_full,
        bias_out_full,
        gain_mid_full,
        shift_mid_full,
        fc_full,
        bias_fc_full,
        down_full,
        bias_down_full,
    ) = gathered
    gain_one = gain_in_full.astype(jnp.float32)
    gain_two = gain_mid_full.astype(jnp.float32)
    device_slot = lax.axis_index("ctx")
    query_pos = block_positions(block_order, device_slot * tokens, tokens, half_block)
    length = cycle_count * tokens
    all_pos = block_positions(block_order, 0, length, half_block)
    owned = head_count // cycle_count
    main_width = owned * cycle_count * HEAD_DIM
    rest_width = model_width - main_width
    own_width = owned * HEAD_DIM

    inputs = block_input.reshape(tokens, model_width)
    wide_in = inputs.astype(jnp.float32)
    hidden_in, normed_in, inv_in = layer_norm(wide_in, gain_one, shift_in_full.astype(jnp.float32))
    act_in = hidden_in.astype(jnp.bfloat16)
    bias_full = jnp.concatenate(
        [
            qv_full[:model_width].astype(jnp.float32),
            jnp.zeros((model_width,), jnp.float32),
            qv_full[model_width:].astype(jnp.float32),
        ]
    )
    qkv_rows = jnp.dot(act_in, qkv_full, preferred_element_type=jnp.float32) + bias_full
    qkv_bf = qkv_rows.astype(jnp.bfloat16)
    thirds = [qkv_bf[:, i * model_width : (i + 1) * model_width] for i in range(3)]
    outgoing = []
    if owned:
        outgoing += [spread(t[:, :main_width], cycle_count) for t in thirds]
    if rest_width:
        outgoing += [
            jnp.broadcast_to(t[None, :, main_width:], (cycle_count, tokens, rest_width))
            for t in thirds[1:]
        ]
    arrived = exchange(jnp.concatenate(outgoing, axis=2)).reshape(length, -1)
    attended_parts = []
    if owned:
        own_q, own_k, own_v = (
            to_heads(arrived[:, i * own_width : (i + 1) * own_width]) for i in range(3)
        )
        own_o, own_lse = attend(own_q, own_k, own_v, all_pos, all_pos, factor)
        back = exchange(from_heads(own_o.astype(jnp.bfloat16)).reshape(cycle_count, tokens, -1))
        attended_parts.append(unspread(back))
    if rest_width:
        rest = arrived[:, 3 * own_width :]
        rest_k, rest_v = to_heads(rest[:, :rest_width]), to_heads(rest[:, rest_width:])
        rest_q = to_heads(thirds[0][:, main_width:])
        rest_o, rest_lse = attend(rest_q, rest_k, rest_v, query_pos, all_pos, factor)
        attended_parts.append(from_heads(rest_o.astype(jnp.bfloat16)))
    attended_bf = jnp.concatenate(attended_parts, axis=1)
    residual = (
        wide_in
        + jnp.dot(attended_bf, out_full, preferred_element_type=jnp.float32)
        + bias_out_full.astype(jnp.float32)
    )
    hidden_mid, normed_mid, inv_mid = layer_norm(
        residual, gain_two, shift_mid_full.astype(jnp.float32)
    )
    act_mid = hidden_mid.astype(jnp.bfloat16)
    pre_act = jnp.dot(act_mid, fc_full, preferred_element_type=jnp.float32) + bias_fc_full.astype(
        jnp.float32
    )
    value_act, slope = gelu_parts(pre_act)
    act_ff = value_act.astype(jnp.bfloat16)
    result = (
        residual
        + jnp.dot(act_ff, down_full.T, preferred_element_type=jnp.float32)
        + bias_down_full.astype(jnp.float32)
    ).astype(jnp.bfloat16)
    qkv_back, out_back, fc_back, down_back = (qkv_full, out_full, fc_full, down_full)
    upstream = cotangent.reshape(tokens, model_width)
    up_wide = upstream.astype(jnp.float32)
    grad_down_bias = jnp.sum(up_wide, axis=0)
    grad_pre = jnp.dot(upstream, down_back, preferred_element_type=jnp.float32) * slope
    grad_fc_bias = jnp.sum(grad_pre, axis=0)
    grad_pre_bf = grad_pre.astype(jnp.bfloat16)
    grad_norm_mid = jnp.dot(grad_pre_bf, fc_back.T, preferred_element_type=jnp.float32)
    grad_gain_mid = jnp.sum(grad_norm_mid * normed_mid, axis=0)
    grad_shift_mid = jnp.sum(grad_norm_mid, axis=0)
    grad_res = up_wide + norm_back(grad_norm_mid, normed_mid, inv_mid, gain_two)
    grad_out_bias = jnp.sum(grad_res, axis=0)
    grad_res_bf = grad_res.astype(jnp.bfloat16)
    grad_heads = jnp.dot(grad_res_bf, out_back.T, preferred_element_type=jnp.float32).astype(
        jnp.bfloat16
    )
    outgoing = []
    if owned:
        own_do = to_heads(exchange(spread(grad_heads[:, :main_width], cycle_count)).reshape(length, -1))
        own_grads = attend_back(
            own_q, own_k, own_v, own_do, own_o, own_lse, all_pos, all_pos, factor
        )
        outgoing += [
            from_heads(g.astype(jnp.bfloat16)).reshape(cycle_count, tokens, -1) for g in own_grads
        ]
    if rest_width:
        rest_dq, rest_dk, rest_dv = attend_back(
            rest_q,
            rest_k,
            rest_v,
            to_heads(grad_heads[:, main_width:]),
            rest_o,
            rest_lse,
            query_pos,
            all_pos,
            factor,
        )
        outgoing += [
            from_heads(g.astype(jnp.bfloat16)).reshape(cycle_count, tokens, -1)
            for g in (rest_dk, rest_dv)
        ]
    arrived = exchange(jnp.concatenate(outgoing, axis=2))
    grads = [[], [], []]
    if owned:
        for i in range(3):
            grads[i].append(unspread(arrived[:, :, i * own_width : (i + 1) * own_width]))
    if rest_width:
        rest = jnp.sum(arrived[:, :, 3 * own_width :].astype(jnp.float32), axis=0)
        grads[0].append(from_heads(rest_dq))
        grads[1].append(rest[:, :rest_width])
        grads[2].append(rest[:, rest_width:])
    grad_query, grad_key, grad_value = (
        jnp.concatenate([p.astype(jnp.bfloat16) for p in parts], axis=1) for parts in grads
    )
    grad_qv_bias = jnp.concatenate(
        [
            jnp.sum(grad_query.astype(jnp.float32), axis=0),
            jnp.sum(grad_value.astype(jnp.float32), axis=0),
        ]
    )
    grad_qkv = jnp.concatenate([grad_query, grad_key, grad_value], axis=1)
    grad_norm_in = jnp.dot(grad_qkv, qkv_back.T, preferred_element_type=jnp.float32)
    grad_gain_in = jnp.sum(grad_norm_in * normed_in, axis=0)
    grad_shift_in = jnp.sum(grad_norm_in, axis=0)
    grad_input = grad_res + norm_back(grad_norm_in, normed_in, inv_in, gain_one)
    column_parts = (
        lax.all_to_all(grad_qkv, "ctx", split_axis=1, concat_axis=0, tiled=True),
        lax.all_to_all(grad_res_bf, "ctx", split_axis=1, concat_axis=0, tiled=True),
        lax.all_to_all(grad_pre_bf, "ctx", split_axis=1, concat_axis=0, tiled=True),
        lax.all_to_all(act_ff, "ctx", split_axis=1, concat_axis=0, tiled=True),
    )
    weight_init = tuple(
        (jnp.zeros((model_width, columns.shape[1]), jnp.float32) for columns in column_parts)
    )
    pieces = (
        lax.all_gather(act_in, "ctx", axis=0, tiled=True),
        lax.all_gather(attended_bf, "ctx", axis=0, tiled=True),
        lax.all_gather(act_mid, "ctx", axis=0, tiled=True),
        lax.all_gather(upstream, "ctx", axis=0, tiled=True),
    )
    updated = []
    for total, piece, columns in zip(weight_init, pieces, column_parts):
        updated.append(jnp.dot(piece.T, columns, preferred_element_type=jnp.float32))
    grad_w_qkv, grad_w_out, grad_w_fc, grad_w_down = tuple(updated)
    vectors = (
        grad_gain_in,
        grad_shift_in,
        grad_qv_bias,
        grad_out_bias,
        grad_gain_mid,
        grad_shift_mid,
        grad_fc_bias,
        grad_down_bias,
    )
    shards = lax.axis_size("fsdp")
    packed = jnp.concatenate([v.reshape(shards, -1) for v in vectors], axis=1)
    packed = lax.psum(packed, ("ctx", "fsdp"))
    packed = lax.dynamic_slice_in_dim(packed, lax.axis_index("fsdp"), 1, axis=0)[0]
    vector_out = []
    offset = 0
    for v in vectors:
        vector_out.append(packed[offset : offset + v.shape[0] // shards])
        offset += v.shape[0] // shards
    summed = tuple(
        lax.psum_scatter(g, "fsdp", scatter_dimension=0, tiled=True)
        for g in (grad_w_qkv, grad_w_out, grad_w_fc, grad_w_down)
    ) + tuple(vector_out)
    return (
        result.reshape(1, tokens, model_width),
        grad_input.reshape(1, tokens, model_width),
        summed[4],
        summed[5],
        summed[0],
        summed[6],
        summed[1],
        summed[7],
        summed[8],
        summed[9],
        summed[2],
        summed[10],
        summed[3],
        summed[11],
    )


def solution(mesh):
    in_specs = (
        P("fsdp", "ctx", None),
        P("fsdp", "ctx", None),
        P(),
        P("fsdp"),
        P("fsdp"),
        P("fsdp", None),
        P("fsdp"),
        P("fsdp", None),
        P("fsdp"),
        P("fsdp"),
        P("fsdp"),
        P("fsdp", None),
        P("fsdp"),
        P("fsdp", None),
        P("fsdp"),
    )
    out_specs = (
        P("fsdp", "ctx", None),
        P("fsdp", "ctx", None),
        P("fsdp"),
        P("fsdp"),
        P("fsdp", "ctx"),
        P("fsdp"),
        P("fsdp", "ctx"),
        P("fsdp"),
        P("fsdp"),
        P("fsdp"),
        P("fsdp", "ctx"),
        P("fsdp"),
        P("fsdp", "ctx"),
        P("fsdp"),
    )
    return jax.shard_map(local, mesh=mesh, in_specs=in_specs, out_specs=out_specs, check_vma=False)
```

time: 1460 us -> 618 us (0.42); the launches traced: 1430 us -> 609 us
  waiting for transfers between devices: 987 us -> 294 us
  matrix products: 134 us -> 59.3 us
  blocking collectives: 85.4 us -> 45.6 us
  Pallas kernels: 0 us -> 33.7 us
  loops' own time: 30.1 us -> 0 us
    ppermute x64 -> x0, waiting for transfers between devices: 749 us -> none  [from_behind(): lax.ppermute(shard, axis, [(i, (i + by) % size) for i in range(size)])]
    all_gather x2 -> x0, waiting for transfers between devices: 177 us -> none  [the longest x1 88.9 us: local(): lax.all_gather(keys_own, 'ctx', axis=0, tiled=True)]
    all_gather x1, waiting for transfers between devices: 0.01 us -> 88.5 us  [local(): lax.all_gather(act_mid, 'ctx', axis=0, tiled=True)]
    all_gather x1, waiting for transfers between devices: 0.02 us -> 81.2 us  [local(): lax.all_gather(attended_bf, 'ctx', axis=0, tiled=True)]
    dot_general x73 -> x0, matrix products: 70.7 us -> none  [the longest x13 14.2 us: cycle_update(): jnp.einsum('hqk,qhe->khe', score_bf, queries, preferred_element_type=jnp....]
    all_to_all x0 -> x4, waiting for transfers between devices: none -> 65.4 us  [exchange(): lax.all_to_all(stacked, 'ctx', split_axis=0, concat_axis=0, tiled=True)]
    ppermute x64 -> x0, starting transfers between devices: 39.4 us -> none  [from_behind(): lax.ppermute(shard, axis, [(i, (i + by) % size) for i in range(size)])]
    psum x1, blocking collectives: 76 us -> 39.3 us  [local(): packed = lax.psum(packed, ('ctx', 'fsdp'))]
  transfers between devices with their start and end apart: 82 -> 20, of which waited for: 39 -> 9; matrix products, arithmetic and copies ran while one was open for 16% -> 22% of each run, Pallas kernels for 0% -> 6%
where the time goes in v1:
time: 618 us; the launch traced here: 609 us
  waiting for transfers between devices  294 us (48%)
  starting transfers between devices  73 us (12%)
  local copies, waits for them, and re-layouts  67.8 us (11%)
  matrix products  59.3 us (10%)
  blocking collectives  45.6 us (7%)
  Pallas kernels  33.7 us (5%)
  other arithmetic  18.7 us (3%)
  between operations  16.9 us (3%)
    all_gather x1, waiting for transfers between devices, local(): lax.all_gather(act_mid, 'ctx', axis=0, tiled=True)  88.5 us
    all_gather x1, waiting for transfers between devices, local(): lax.all_gather(attended_bf, 'ctx', axis=0, tiled=True)  81.2 us
    all_to_all x4, waiting for transfers between devices, exchange(): lax.all_to_all(stacked, 'ctx', split_axis=0, concat_axis=0, tiled=True)  65.4 us
    psum x1, blocking collectives, local(): packed = lax.psum(packed, ('ctx', 'fsdp'))  39.3 us
    all_to_all x1, waiting for transfers between devices, local(): lax.all_to_all(act_ff, 'ctx', split_axis=1, concat_axis=0, tiled=True)  32.2 us
    unnamed x132, local copies, waits for them, and re-layouts  31.7 us
    all_to_all x4, starting transfers between devices, exchange(): lax.all_to_all(stacked, 'ctx', split_axis=0, concat_axis=0, tiled=True)  26.9 us
    pallas_call x2, Pallas kernels, attend_back(): pl.pallas_call(functools.partial(attend_back_kernel, factor), grid=(heads...  23.4 us
  transfers between devices with their start and end apart: 20, of which 9 were waited for; matrix products, arithmetic and copies ran while one was open for 22% of the time, Pallas kernels for 6%

profile of v1, /device:TPU:0, one launch (start us, length us, event | category | flops | bytes accessed | tf_op | source)
XLA Modules:
  0.0 608.6 jit_solution(3714852119660978969)
XLA Ops:
  14.4 4.3 all-reduce.7
  20.5 9.9 %all-gather.11.cloned.1.call-done = bf16[1088,3264]{1,0:T(8,128)(2,1)} async-done(((bf16[544,3264]{1,0:T(8,128)(2,1)}), bf16[1088,3264]{1,0:T(8,128)(2,1)}) %all-gather.11.cloned.1.call-update) | async-done | bytes 7102480 | tf_op jit(solution)/shard_map/all_gather | solution.py:210
  30.5 4.5 fusion
  39.8 6.8 %all-to-all-start = ((bf16[16,128,320]{1,2,0:T(8,128)(2,1)}), bf16[16,128,320]{1,2,0:T(8,128)(2,1)S(1)}, u32[]{:S(2)}, u32[]{:S(2)}) async-start(bf16[16,128,320]{1,2,0:T(8,128)(2,1)} %broadcast_dynamic-update-slice_fusion), calls=%async_computation | async-start | bytes 2621440 | tf_op jit(solution)/shard_map/all_to_all | solution.py:181
  46.7 1.4 copy.97
  48.2 1.3 fusion.20.qpos_ref
  49.6 26.6 %all-to-all-done = bf16[16,128,320]{1,2,0:T(8,128)(2,1)S(1)} async-done(((bf16[16,128,320]{1,2,0:T(8,128)(2,1)}), bf16[16,128,320]{1,2,0:T(8,128)(2,1)S(1)}, u32[]{:S(2)}, u32[]{:S(2)}) %all-to-all-start) | async-done | bytes 1310752 | tf_op jit(solution)/shard_map/all_to_all | solution.py:181
  76.2 1.5 copy.96
  77.7 2.5 slice_bitcast_fusion.2
  80.3 9.5 %shard_map.254 = (f32[1,2048,64]{2,1,0:T(8,128)S(1)}, f32[1,2048,1]{2,1,0:T(8,128)S(1)}) custom-call(bf16[1,2048,64]{2,1,0:T(8,128)(2,1)S(1)} %get-tuple-element.63.q_ref, bf16[1,2048,64]{2,1,0:T(8,128)(2,1)S(1)} %get-tuple-element.62.k_ref, bf16[1,2048,64]{2,1,0:T(8,128)(2,1)S(1)} %get-tuple-element.59.v_ref, s32[2048,1]{1,0:T(8,128)S(1)} %fusion.20.qpos_ref, ...), custom_call_target="tpu_custom_call" | custom-call | flops 1073741824 | bytes 1572864 | tf_op jit(solution)/shard_map/pallas_call | solution.py:122
  91.8 7.3 %all-to-all-start.1 = ((bf16[16,128,64]{1,2,0:T(8,128)(2,1)}), bf16[16,128,64]{1,2,0:T(8,128)(2,1)S(1)}, u32[]{:S(2)}, u32[]{:S(2)}) async-start(bf16[16,128,64]{1,2,0:T(8,128)(2,1)} %copy.98), calls=%async_computation.1 | async-start | bytes 524288 | tf_op jit(solution)/shard_map/all_to_all | solution.py:181
  100.3 7.8 %all-to-all-done.1 = bf16[16,128,64]{1,2,0:T(8,128)(2,1)S(1)} async-done(((bf16[16,128,64]{1,2,0:T(8,128)(2,1)}), bf16[16,128,64]{1,2,0:T(8,128)(2,1)S(1)}, u32[]{:S(2)}, u32[]{:S(2)}) %all-to-all-start.1) | async-done | bytes 262176 | tf_op jit(solution)/shard_map/all_to_all | solution.py:181
  108.9 2.0 all-gather.1
  111.0 2.9 fusion.56
  115.2 7.4 %multiply_convert_fusion = (bf16[128,4352]{1,0:T(8,128)(2,1)S(1)}, f32[128,4352]{1,0:T(8,128)}) fusion(f32[4352]{0:T(1024)S(1)} %reshape.356, bf16[128,1088]{0,1:T(8,128)(2,1)} %add_convert_fusion, bf16[1088,4352]{1,0:T(8,128)(2,1)} %all-gather.15.cloned.1.call-done), kind=kOutput, calls=%fused_computation.21 | convolution fusion | flops 1217724416 | bytes 13108224 | tf_op jit(solution)/shard_map/dot_general | solution.py:293
  122.6 7.4 %fusion.51 = (f32[4352]{0:T(1024)S(1)}, bf16[128,4352]{1,0:T(8,128)(2,1)S(1)}) fusion(f32[128,4352]{1,0:T(8,128)} %get-tuple-element.81, bf16[1088,4352]{1,0:T(8,128)(2,1)} %all-gather.17.cloned.1.call-done, bf16[1,128,1088]{1,2,0:T(8,128)(2,1)} %param.16), kind=kOutput, calls=%fused_computation.140 | convolution fusion | flops 1223290624 | bytes 13108224 | tf_op jit(solution)/shard_map/dot_general | solution.py:307
  130.1 2.8 multiply_reduce_fusion
  137.3 4.4 all-to-all-start.2
  141.7 1.4 slice_bitcast_fusion.5.do_ref
  143.1 3.6 shard_map.257
  146.7 2.1 convert_element_type.125
  148.8 1.3 copy.107
  150.1 2.1 convert_element_type.126
  152.2 1.9 copy.108
  154.1 2.0 copy.103
  156.1 19.8 %shard_map.256 = (f32[1,2048,64]{2,1,0:T(8,128)}, f32[1,2048,64]{2,1,0:T(8,128)}, f32[1,2048,64]{2,1,0:T(8,128)}) custom-call(bf16[1,2048,64]{2,1,0:T(8,128)(2,1)} %copy-done.7, bf16[1,2048,64]{2,1,0:T(8,128)(2,1)} %copy-done.6, bf16[1,2048,64]{2,1,0:T(8,128)(2,1)} %copy-done.5, bf16[1,2048,64]{2,1,0:T(8,128)(2,1)} %bitcast.196, f32[1,2048,64]{2,1,0:T(8,128)} %copy-done.2, ...), custom_call_target="tpu_custom_call" | custom-call | flops 2684354560 | bytes 3670016 | tf_op jit(solution)/shard_map/pallas_call | solution.py:145
  175.9 2.1 convert_element_type.122
  178.0 1.9 copy.104
  179.9 2.1 convert_element_type.123
  182.0 1.9 copy.105
  183.9 2.1 convert_element_type.124
  186.0 1.9 copy.106
  188.0 1.8 constant_dynamic-update-slice_fusion.7
  189.7 1.7 constant_dynamic-update-slice_fusion.6
  191.4 1.7 constant_dynamic-update-slice_fusion.5
  194.7 8.4 %all-to-all-start.3 = ((bf16[16,128,320]{1,2,0:T(8,128)(2,1)}), bf16[16,128,320]{1,2,0:T(8,128)(2,1)}, u32[]{:S(2)}, u32[]{:S(2)}) async-start(bf16[16,128,320]{1,2,0:T(8,128)(2,1)} %constant_dynamic-update-slice_fusion.3), calls=%async_computation.3 | async-start | bytes 2621440 | tf_op jit(solution)/shard_map/all_to_all | solution.py:181
  203.1 1.4 copy.115
  204.6 31.0 %all-to-all-done.3 = bf16[16,128,320]{1,2,0:T(8,128)(2,1)} async-done(((bf16[16,128,320]{1,2,0:T(8,128)(2,1)}), bf16[16,128,320]{1,2,0:T(8,128)(2,1)}, u32[]{:S(2)}, u32[]{:S(2)}) %all-to-all-start.3) | async-done | bytes 1310752 | tf_op jit(solution)/shard_map/all_to_all | solution.py:181
  235.6 19.7 %all-to-all-start.7 = ((bf16[128,16,272]{0,2,1:T(8,128)(2,1)}), bf16[128,16,272]{0,2,1:T(8,128)(2,1)}, u32[]{:S(2)}, u32[]{:S(2)}) async-start(bf16[128,16,272]{0,2,1:T(8,128)(2,1)} %bitcast.173), calls=%async_computation.7 | async-start | bytes 2228224 | tf_op jit(solution)/shard_map/all_to_all | solution.py:372
  255.4 1.2 fusion.52
  262.4 2.0 all_to_all.72
  264.4 32.2 %all-to-all-done.7 = bf16[128,16,272]{0,2,1:T(8,128)(2,1)} async-done(((bf16[128,16,272]{0,2,1:T(8,128)(2,1)}), bf16[128,16,272]{0,2,1:T(8,128)(2,1)}, u32[]{:S(2)}, u32[]{:S(2)}) %all-to-all-start.7) | async-done | bytes 1114144 | tf_op jit(solution)/shard_map/all_to_all | solution.py:372
  296.6 16.7 %all-to-all-start.4 = ((bf16[128,16,204]{0,2,1:T(8,128)(2,1)}), bf16[128,16,204]{0,2,1:T(8,128)(2,1)}, u32[]{:S(2)}, u32[]{:S(2)}) async-start(bf16[128,16,204]{0,2,1:T(8,128)(2,1)} %all_to_all.72), calls=%async_computation.4 | async-start | bytes 1703936 | tf_op jit(solution)/shard_map/all_to_all | solution.py:369
  313.3 5.3 fusion.3
  318.6 3.0 copy.125
  321.6 1.7 all_to_all.76
  323.4 8.4 %all-to-all-done.4 = bf16[128,16,204]{0,2,1:T(8,128)(2,1)} async-done(((bf16[128,16,204]{0,2,1:T(8,128)(2,1)}), bf16[128,16,204]{0,2,1:T(8,128)(2,1)}, u32[]{:S(2)}, u32[]{:S(2)}) %all-to-all-start.4) | async-done | bytes 835616 | tf_op jit(solution)/shard_map/all_to_all | solution.py:369
  331.8 4.6 all-to-all-start.5
  336.4 1.4 copy.113
  337.8 1.4 copy.141
  340.5 4.8 all-to-all-done.5
  345.3 4.4 all-to-all-start.6
  349.7 4.6 fusion.57
  355.8 81.2 %all-gather.21.cloned.1.call-done = bf16[2048,1088]{0,1:T(8,128)(2,1)} async-done(((bf16[128,1088]{0,1:T(8,128)(2,1)}), bf16[2048,1088]{0,1:T(8,128)(2,1)}) %all-gather.21.cloned.1.call-update) | async-done | bytes 4456464 | tf_op jit(solution)/shard_map/all_gather | solution.py:379
  437.0 4.4 fusion.58
  441.8 88.5 %all-gather.23.cloned.1.call-done = bf16[2048,1088]{0,1:T(8,128)(2,1)} async-done(((bf16[128,1088]{0,1:T(8,128)(2,1)}), bf16[2048,1088]{0,1:T(8,128)(2,1)}) %all-gather.23.cloned.1.call-update) | async-done | bytes 4456464 | tf_op jit(solution)/shard_map/all_gather | solution.py:380
  530.3 6.3 %fusion.17 = f32[1088,272]{1,0:T(8,128)} fusion(bf16[2048,1088]{0,1:T(8,128)(2,1)} %all-gather.23.cloned.1.call-done, bf16[128,16,272]{0,2,1:T(8,128)(2,1)} %all-to-all-done.6), kind=kOutput, calls=%fused_computation.25 | convolution fusion | flops 1212153856 | bytes 6754304
  536.6 7.4 %fusion.9 = bf16[1,128,1088]{1,2,0:T(8,128)(2,1)} fusion(f32[128,1088]{0,1:T(8,128)S(1)} %get-tuple-element.79, bf16[128,4352]{1,0:T(8,128)(2,1)S(1)} %get-tuple-element.80, bf16[1088,4352]{1,0:T(8,128)(2,1)} %all-gather.17.cloned.1.call-done, f32[1088]{0:T(1024)S(1)} %convert_element_type.116), kind=kOutput, calls=%fused_computation.15 | convolution fusion | flops 1212571648 | bytes 11424000 | tf_op jit(solution)/shard_map/dot_general | solution.py:300
  544.1 5.5 fusion.38
  550.4 39.3 %psum.7 = f32[2,6528]{1,0:T(2,128)S(1)} all-reduce(f32[2,6528]{1,0:T(2,128)S(1)} %concatenate.36), channel_id=1, replica_groups=mesh['ctx'=16,'fsdp'=2] {'ctx','fsdp'}, use_global_device_ids=true, to_apply=%region_20.21 | all-reduce | flops 13056 | bytes 104448 | tf_op jit(solution)/shard_map/psum | solution.py:399
  592.8 2.3 copy.126
  595.2 2.1 copy.120
  597.2 1.8 copy.122
  599.0 2.3 copy.124
  (232 shorter events, 36.9 us)
Async XLA Ops:
  7.2 23.3 %all-gather.11.cloned.1.call-start = ((), (), s32[]{:S(2)}) async-start(), calls=%async_computation.12 | async-start | bytes 10862592 | tf_op jit(solution)/shard_map/all_gather | solution.py:210
  7.9 103.1 %all-gather.13.cloned.1.call-start = ((), (), s32[]{:S(2)}) async-start(), calls=%async_computation.13 | async-start | bytes 3760128 | tf_op jit(solution)/shard_map/all_gather | solution.py:212
  8.7 106.6 %all-gather.15.cloned.1.call-start = ((), (), s32[]{:S(2)}) async-start(), calls=%async_computation.14 | async-start | bytes 14204928 | tf_op jit(solution)/shard_map/all_gather | solution.py:216
  9.4 1.3 copy-start.46
  9.4 3.2 copy-start.39
  9.4 3.5 copy-start.40
  9.4 3.7 copy-start.41
  9.4 3.9 copy-start.42
  9.5 4.2 copy-start.43
  9.5 4.4 copy-start.44
  9.5 4.6 copy-start.36
  9.5 9.2 %copy-start.15 = (bf16[1,128,1088]{1,2,0:T(8,128)(2,1)S(1)}, bf16[1,128,1088]{1,2,0:T(8,128)(2,1)}, u32[]{:S(2)}) copy-start(bf16[1,128,1088]{1,2,0:T(8,128)(2,1)} %param.15) | copy-start | bytes 835588
  9.5 113.1 %all-gather.17.cloned.1.call-start = ((), (), s32[]{:S(2)}) async-start(), calls=%async_computation.15 | async-start | bytes 14204928 | tf_op jit(solution)/shard_map/all_gather | solution.py:218
  10.1 303.2 %all-gather.25.cloned.1.call-start = ((), (), s32[]{:S(2)}) async-start(), calls=%async_computation.19 | async-start | bytes 4734976 | tf_op jit(solution)/shard_map/all_gather | solution.py:381
  10.7 339.1 %all-gather.19.cloned.1.call-start = ((), (), s32[]{:S(2)}) async-start(), calls=%async_computation.16 | async-start | bytes 4734976 | tf_op jit(solution)/shard_map/all_gather | solution.py:378
  18.8 1.7 copy-start.33
  19.3 1.3 copy-start.37
  35.7 63.7 %copy-start.8 = (bf16[1,128,64]{2,1,0:T(8,128)(2,1)}, bf16[1,128,64]{2,1,0:T(8,128)(2,1)S(1)}, u32[]{:S(2)}) copy-start(bf16[1,128,64]{2,1,0:T(8,128)(2,1)S(1)} %get-tuple-element.68.q_ref) | copy-start | bytes 49156
  36.7 9.9 %copy-start.45 = (s32[32]{0:T(128)S(1)}, s32[32]{0:T(128)}, u32[]{:S(2)}) copy-start(s32[32]{0:T(128)} %param.17) | copy-start | bytes 388
  39.8 36.4 %all-to-all-start = ((bf16[16,128,320]{1,2,0:T(8,128)(2,1)}), bf16[16,128,320]{1,2,0:T(8,128)(2,1)S(1)}, u32[]{:S(2)}, u32[]{:S(2)}) async-start(bf16[16,128,320]{1,2,0:T(8,128)(2,1)} %broadcast_dynamic-update-slice_fusion), calls=%async_computation | async-start | bytes 2621440 | tf_op jit(solution)/shard_map/all_to_all | solution.py:181
  48.2 51.2 %copy-start.10 = (s32[1,2048]{1,0:T(1,128)}, s32[1,2048]{1,0:T(1,128)S(1)}, u32[]{:S(2)}) copy-start(s32[1,2048]{1,0:T(1,128)S(1)} %fusion.46.kpos_ref) | copy-start | bytes 24580
  49.6 30.7 %copy-start.3 = (s32[2048,1]{1,0:T(8,128)}, s32[2048,1]{1,0:T(8,128)S(1)}, u32[]{:S(2)}) copy-start(s32[2048,1]{1,0:T(8,128)S(1)} %fusion.20.qpos_ref) | copy-start | bytes 24580
  80.2 9.6 %copy-start.5 = (bf16[1,2048,64]{2,1,0:T(8,128)(2,1)}, bf16[1,2048,64]{2,1,0:T(8,128)(2,1)S(1)}, u32[]{:S(2)}) copy-start(bf16[1,2048,64]{2,1,0:T(8,128)(2,1)S(1)} %get-tuple-element.59.v_ref) | copy-start | bytes 786436
  80.3 9.6 %copy-start.6 = (bf16[1,2048,64]{2,1,0:T(8,128)(2,1)}, bf16[1,2048,64]{2,1,0:T(8,128)(2,1)S(1)}, u32[]{:S(2)}) copy-start(bf16[1,2048,64]{2,1,0:T(8,128)(2,1)S(1)} %get-tuple-element.62.k_ref) | copy-start | bytes 786436
  80.3 9.6 %copy-start.7 = (bf16[1,2048,64]{2,1,0:T(8,128)(2,1)}, bf16[1,2048,64]{2,1,0:T(8,128)(2,1)S(1)}, u32[]{:S(2)}) copy-start(bf16[1,2048,64]{2,1,0:T(8,128)(2,1)S(1)} %get-tuple-element.63.q_ref) | copy-start | bytes 786436
  80.3 19.1 %copy-start = (bf16[1,2048,64]{2,1,0:T(8,128)(2,1)}, bf16[1,2048,64]{2,1,0:T(8,128)(2,1)S(1)}, u32[]{:S(2)}) copy-start(bf16[1,2048,64]{2,1,0:T(8,128)(2,1)S(1)} %get-tuple-element.60.v_ref) | copy-start | bytes 786436
  80.3 19.1 %copy-start.1 = (bf16[1,2048,64]{2,1,0:T(8,128)(2,1)}, bf16[1,2048,64]{2,1,0:T(8,128)(2,1)S(1)}, u32[]{:S(2)}) copy-start(bf16[1,2048,64]{2,1,0:T(8,128)(2,1)S(1)} %get-tuple-element.61.k_ref) | copy-start | bytes 786436
  89.9 1.0 copy-start.12
  90.8 18.0 %copy-start.2 = (f32[1,2048,64]{2,1,0:T(8,128)}, f32[1,2048,64]{2,1,0:T(8,128)S(1)}, u32[]{:S(2)}) copy-start(f32[1,2048,64]{2,1,0:T(8,128)S(1)} %get-tuple-element.24.o_ref) | copy-start | bytes 1572868
  90.9 18.0 %copy-start.32 = (bf16[2176]{0:T(1024)(128)(2,1)S(1)}, bf16[2176]{0:T(1024)(128)(2,1)}, u32[]{:S(2)}) copy-start(bf16[2176]{0:T(1024)(128)(2,1)} %param.27) | copy-start | bytes 13060
  90.9 20.1 %copy-start.16 = (bf16[1,128,1088]{1,2,0:T(8,128)(2,1)S(1)}, bf16[1,128,1088]{1,2,0:T(8,128)(2,1)}, u32[]{:S(2)}) copy-start(bf16[1,128,1088]{1,2,0:T(8,128)(2,1)} %param.15) | copy-start | bytes 835588
  91.8 16.2 %all-to-all-start.1 = ((bf16[16,128,64]{1,2,0:T(8,128)(2,1)}), bf16[16,128,64]{1,2,0:T(8,128)(2,1)S(1)}, u32[]{:S(2)}, u32[]{:S(2)}) async-start(bf16[16,128,64]{1,2,0:T(8,128)(2,1)} %copy.98), calls=%async_computation.1 | async-start | bytes 524288 | tf_op jit(solution)/shard_map/all_to_all | solution.py:181
  99.2 337.8 %all-gather.21.cloned.1.call-start = ((), (), s32[]{:S(2)}) async-start(), calls=%async_computation.17 | async-start | bytes 4734976 | tf_op jit(solution)/shard_map/all_gather | solution.py:379
  99.4 14.5 %copy-start.4 = (s32[128,1]{1,0:T(8,128)}, s32[128,1]{1,0:T(8,128)S(1)}, u32[]{:S(2)}) copy-start(s32[128,1]{1,0:T(8,128)S(1)} %fusion.42.qpos_ref) | copy-start | bytes 1540
  100.2 13.7 %copy-start.9 = (f32[1,128,64]{2,1,0:T(8,128)}, f32[1,128,64]{2,1,0:T(8,128)S(1)}, u32[]{:S(2)}) copy-start(f32[1,128,64]{2,1,0:T(8,128)S(1)} %get-tuple-element.25.o_ref) | copy-start | bytes 98308
  100.2 13.7 %copy-start.11 = (f32[1,128,1]{2,1,0:T(8,128)}, f32[1,128,1]{2,1,0:T(8,128)S(1)}, u32[]{:S(2)}) copy-start(f32[1,128,1]{2,1,0:T(8,128)S(1)} %get-tuple-element.30.lse_ref) | copy-start | bytes 1540
  108.8 421.5 %all-gather.23.cloned.1.call-start = ((), (), s32[]{:S(2)}) async-start(), calls=%async_computation.18 | async-start | bytes 4734976 | tf_op jit(solution)/shard_map/all_gather | solution.py:380
  122.6 7.5 %copy-start.13 = (bf16[1088,4352]{1,0:T(8,128)(2,1)S(1)}, bf16[1088,4352]{1,0:T(8,128)(2,1)}, u32[]{:S(2)}) copy-start(bf16[1088,4352]{1,0:T(8,128)(2,1)} %all-gather.15.cloned.1.call-done) | copy-start | bytes 28409860
  130.1 2.8 copy-start.23
  132.9 1.9 copy-start.14
  133.4 0.8 copy-start.17
  134.8 0.9 copy-start.19
  137.3 16.8 %all-to-all-start.2 = ((bf16[16,128,64]{1,2,0:T(8,128)(2,1)}), bf16[16,128,64]{1,2,0:T(8,128)(2,1)}, u32[]{:S(2)}, u32[]{:S(2)}) async-start(bf16[16,128,64]{1,2,0:T(8,128)(2,1)} %bitcast.26), calls=%async_computation.2 | async-start | bytes 524288 | tf_op jit(solution)/shard_map/all_to_all | solution.py:181
  188.0 6.0 copy-start.24
  194.7 40.9 %all-to-all-start.3 = ((bf16[16,128,320]{1,2,0:T(8,128)(2,1)}), bf16[16,128,320]{1,2,0:T(8,128)(2,1)}, u32[]{:S(2)}, u32[]{:S(2)}) async-start(bf16[16,128,320]{1,2,0:T(8,128)(2,1)} %constant_dynamic-update-slice_fusion.3), calls=%async_computation.3 | async-start | bytes 2621440 | tf_op jit(solution)/shard_map/all_to_all | solution.py:181
  203.1 52.2 %copy-start.31 = (f32[1,128,64]{2,1,0:T(8,128)S(1)}, f32[1,128,64]{2,1,0:T(8,128)}, u32[]{:S(2)}) copy-start(f32[1,128,64]{2,1,0:T(8,128)} %get-tuple-element.33) | copy-start | bytes 98308
  235.6 61.0 %all-to-all-start.7 = ((bf16[128,16,272]{0,2,1:T(8,128)(2,1)}), bf16[128,16,272]{0,2,1:T(8,128)(2,1)}, u32[]{:S(2)}, u32[]{:S(2)}) async-start(bf16[128,16,272]{0,2,1:T(8,128)(2,1)} %bitcast.173), calls=%async_computation.7 | async-start | bytes 2228224 | tf_op jit(solution)/shard_map/all_to_all | solution.py:372
  255.4 9.0 %copy-start.26 = (bf16[128,64]{0,1:T(8,128)(2,1)}, bf16[128,64]{0,1:T(8,128)(2,1)S(1)}, u32[]{:S(2)}) copy-start(bf16[128,64]{0,1:T(8,128)(2,1)S(1)} %copy.109) | copy-start | bytes 49156
  296.6 35.2 %all-to-all-start.4 = ((bf16[128,16,204]{0,2,1:T(8,128)(2,1)}), bf16[128,16,204]{0,2,1:T(8,128)(2,1)}, u32[]{:S(2)}, u32[]{:S(2)}) async-start(bf16[128,16,204]{0,2,1:T(8,128)(2,1)} %all_to_all.72), calls=%async_computation.4 | async-start | bytes 1703936 | tf_op jit(solution)/shard_map/all_to_all | solution.py:369
  313.2 279.6 %reduce-scatter.19.cloned.1.call-start = ((), (), s32[]{:S(2)}) async-start(), calls=%async_computation.23 | async-start | bytes 2506752
  331.8 13.5 %all-to-all-start.5 = ((bf16[128,16,68]{0,2,1:T(8,128)(2,1)}), bf16[128,16,68]{0,2,1:T(8,128)(2,1)}, u32[]{:S(2)}, u32[]{:S(2)}) async-start(bf16[128,16,68]{0,2,1:T(8,128)(2,1)} %all_to_all.76), calls=%async_computation.5 | async-start | bytes 589824 | tf_op jit(solution)/shard_map/all_to_all | solution.py:370
  340.5 9.3 %copy-start.25 = (bf16[26,8,16,128]{3,1,2,0:T(8,128)(2,1)S(1)}, bf16[26,8,16,128]{3,1,2,0:T(8,128)(2,1)}, u32[]{:S(2)}) copy-start(bf16[26,8,16,128]{3,1,2,0:T(8,128)(2,1)} %copy.129) | copy-start | bytes 2555908
  345.3 96.6 %all-to-all-start.6 = ((bf16[128,16,272]{0,2,1:T(8,128)(2,1)}), bf16[128,16,272]{0,2,1:T(8,128)(2,1)}, u32[]{:S(2)}, u32[]{:S(2)}) async-start(bf16[128,16,272]{0,2,1:T(8,128)(2,1)} %bitcast.46), calls=%async_computation.6 | async-start | bytes 2228224 | tf_op jit(solution)/shard_map/all_to_all | solution.py:371
  349.7 245.5 %reduce-scatter.13.cloned.1.call-start = ((), (), s32[]{:S(2)}) async-start(), calls=%async_computation.20 | async-start | bytes 1671168
  354.4 242.8 %reduce-scatter.15.cloned.1.call-start = ((), (), s32[]{:S(2)}) async-start(), calls=%async_computation.21 | async-start | bytes 835584
  437.0 4.5 copy-start.35
  441.4 157.6 %reduce-scatter.17.cloned.1.call-start = ((), (), s32[]{:S(2)}) async-start(), calls=%async_computation.22 | async-start | bytes 2506752
  536.6 7.4 %copy-start.29 = (f32[1088]{0:T(1024)S(1)}, f32[1088]{0:T(1024)}, u32[]{:S(2)}) copy-start(f32[1088]{0:T(1024)} %copy-done.28) | copy-start | bytes 13060
  536.6 7.4 %copy-start.34 = (f32[128]{0:T(128)S(1)}, f32[128]{0:T(128)}, u32[]{:S(2)}) copy-start(f32[128]{0:T(128)} %copy-done.33) | copy-start | bytes 1540
  536.6 7.4 %copy-start.38 = (f32[128]{0:T(128)S(1)}, f32[128]{0:T(128)}, u32[]{:S(2)}) copy-start(f32[128]{0:T(128)} %copy-done.37) | copy-start | bytes 1540
  544.0 5.7 copy-start.21
  544.0 5.7 copy-start.27
  544.0 5.8 copy-start.30
  544.1 47.8 %copy-start.18 = (f32[128,1088]{0,1:T(8,128)S(1)}, f32[128,1088]{0,1:T(8,128)}, u32[]{:S(2)}) copy-start(f32[128,1088]{0,1:T(8,128)} %copy-done.17) | copy-start | bytes 1671172
  (3 other events, 2.0 us)
Sparse Core Ops, SparseCore 0:
  9.6 20.8 all-gather.10
  32.0 12.3 all-gather.12
  45.9 23.0 all-gather.14
  70.4 23.0 all-gather.16
  96.1 94.6 all-gather.24
  193.9 132.3 all-gather.18
  329.1 107.8 all-gather.20
  439.7 90.5 all-gather.22
  532.6 7.3 reduce-scatter.18
  542.0 9.8 reduce-scatter.12
  554.9 9.0 reduce-scatter.14
  566.2 10.3 reduce-scatter.16
